TPU v7x, 512 devices: a whole 4x8x8 slice. The times are simulated.
512 devices in a mesh: gx: 8 (over y), gy: 16 (over z, core), gz: 4 (over x).
Axes of the slice: x: 4, y: 8, z: 8, core: 2. Of those that a mesh axis runs over, the one named last changes fastest.
Arguments:
- source: float32 [2, 64, 256, 1024], P(None, 'gz', 'gy', 'gx'), may hold values from -6 to 6
- adjoint_guess: float32 [2, 64, 256, 1024], P(None, 'gz', 'gy', 'gx'), may hold values from -6 to 6
- forward_field: float32 [2, 64, 256, 1024], P(None, 'gz', 'gy', 'gx'), may hold values from -6 to 6
- labels: int32 [64, 256, 1024], P('gz', 'gy', 'gx'), may hold values from 0 to 7
- perm_real: float32 [8], replicated, may hold values from 1 to 4
- perm_imag: float32 [8], replicated, may hold values from 0 to 1
Outputs:
- adjoint: float32 [2, 64, 256, 1024], P(None, 'gz', 'gy', 'gx')
- material_grad: float32 [2, 8], replicated
- norms: float32 [3], replicated
All inputs are finite; a program needn't handle non-finite values.
Results may differ from a plain program's by a relative error of at most 0.0001.
Values sent between devices are 32-bit elements; how exact they have to be, the bound alone decides.
A program may use at most 64 MiB of HBM per device.

v0:
```python
import jax
import jax.numpy as jnp
from jax import lax
from jax.sharding import PartitionSpec as P

NMAT = 8
SWEEPS = 3


KH2 = 0.5
SHIFT = 0.5
DAMP = 0.5


def extended(block, sides, width):
    for axis, dim in sides:
        count = lax.axis_size(axis)
        forward = [(i, i + 1) for i in range(count - 1)]
        backward = [(target, source) for source, target in forward]
        low = lax.ppermute(
            lax.slice_in_dim(block, block.shape[dim] - width, None, axis=dim), axis, forward
        )
        high = lax.ppermute(lax.slice_in_dim(block, 0, width, axis=dim), axis, backward)
        block = jnp.concatenate([low, block, high], axis=dim)
    return block


def cmul(left, right):
    return jnp.stack(
        [left[0] * right[0] - left[1] * right[1], left[0] * right[1] + left[1] * right[0]]
    )


def neighbours(padded):
    total = padded[:, 2:, 1:-1, 1:-1] + padded[:, :-2, 1:-1, 1:-1]
    total = total + padded[:, 1:-1, 2:, 1:-1] + padded[:, 1:-1, :-2, 1:-1]
    return total + padded[:, 1:-1, 1:-1, 2:] + padded[:, 1:-1, 1:-1, :-2]


def coefficients(labels, perm_real, perm_imag):
    eps_re = jnp.zeros(labels.shape, jnp.float32)
    eps_im = jnp.zeros(labels.shape, jnp.float32)
    for material in range(perm_real.shape[0]):
        chosen = labels == material
        eps_re = eps_re + jnp.where(chosen, perm_real[material], 0.0)
        eps_im = eps_im + jnp.where(chosen, perm_imag[material], 0.0)
    shift_re = KH2 * (eps_re + SHIFT * eps_im)
    shift_im = KH2 * (SHIFT * eps_re - eps_im)
    diag_re = 6.0 - shift_re
    diag_im = -shift_im
    denom = diag_re * diag_re + diag_im * diag_im
    shifts = jnp.stack([shift_re, shift_im])
    inverse = jnp.stack([diag_re / denom, -diag_im / denom])
    return (shifts, inverse, eps_re)


def fine_residual(source, field, shifts):
    padded = extended(field, (("gx", 3), ("gy", 2), ("gz", 1)), 1)
    return source - (6.0 * field - neighbours(padded) - cmul(shifts, field))


def coarse_step(coarse, padded, rhs, inv_c, coarse_q):
    near = neighbours(padded)
    real_part = 6.0 * coarse[0] - near[0] - 4.0 * coarse_q * coarse[1]
    imag_part = 6.0 * coarse[1] - near[1] + 4.0 * coarse_q * coarse[0]
    return coarse + DAMP * cmul(inv_c, rhs - jnp.stack([real_part, imag_part]))


def restrict(field):
    lead = field.shape[:-3]
    zlen, ylen, xlen = field.shape[-3:]
    blocks = field.reshape(lead + (zlen // 2, 2, ylen // 2, 2, xlen // 2, 2))
    return jnp.mean(blocks, axis=(-5, -3, -1))


def prolong(field):
    field = jnp.repeat(field, 2, axis=-1)
    field = jnp.repeat(field, 2, axis=-2)
    return jnp.repeat(field, 2, axis=-3)


def coarse_inverse(coarse_q):
    denom = 36.0 + 16.0 * coarse_q * coarse_q
    return jnp.stack([6.0 / denom, -4.0 * coarse_q / denom])


def shards(source, adjoint_guess, forward_field, labels, perm_real, perm_imag):
    shifts, inverse, eps_re = coefficients(labels, perm_real, perm_imag)
    field = adjoint_guess
    for sweep in range(SWEEPS):
        field = field + DAMP * cmul(inverse, fine_residual(source, field, shifts))
    r_pre = fine_residual(source, field, shifts)
    source_sq = jnp.sum(source * source)
    pre_sq = jnp.sum(r_pre * r_pre)
    source_sq, pre_sq = lax.psum((source_sq, pre_sq), ("gx", "gy", "gz"))
    rhs = 4.0 * restrict(r_pre)
    coarse_q = restrict(KH2 * eps_re)
    inv_c = coarse_inverse(coarse_q)
    coarse = DAMP * cmul(inv_c, rhs)
    padded = extended(coarse, (("gx", 3), ("gy", 2), ("gz", 1)), 1)
    coarse = coarse_step(coarse, padded, rhs, inv_c, coarse_q)
    adjoint = field + prolong(coarse)
    r_fin = fine_residual(source, adjoint, shifts)
    fin_sq = jnp.sum(r_fin * r_fin)
    product = cmul(forward_field, adjoint)
    sums = []
    for material in range(NMAT):
        chosen = labels == material
        sums.append(
            jnp.stack(
                [
                    jnp.sum(jnp.where(chosen, product[0], 0.0)),
                    jnp.sum(jnp.where(chosen, product[1], 0.0)),
                ]
            )
        )
    grad_sums = jnp.stack(sums, axis=1)
    fin_sq, grad_sums = lax.psum((fin_sq, grad_sums), ("gx", "gy", "gz"))
    count = (
        lax.axis_size("gx")
        * lax.axis_size("gy")
        * lax.axis_size("gz")
        * labels.shape[0]
        * labels.shape[1]
        * labels.shape[2]
    )
    cells = float(count)
    norms = jnp.sqrt(jnp.stack([source_sq, pre_sq, fin_sq]) / cells)
    material_grad = -KH2 / cells**0.5 * grad_sums
    return (adjoint, material_grad, norms)


def solution(mesh):
    return jax.shard_map(
        shards,
        mesh=mesh,
        in_specs=(
            P(None, "gz", "gy", "gx"),
            P(None, "gz", "gy", "gx"),
            P(None, "gz", "gy", "gx"),
            P("gz", "gy", "gx"),
            P(),
            P(),
        ),
        out_specs=(P(None, "gz", "gy", "gx"), P(), P()),
        check_vma=False,
    )
```

profile of v0, /device:TPU:1, one launch (start us, length us, event | category | flops | bytes accessed | tf_op | source)
XLA Modules:
  0.0 338.8 jit_solution(17374778045524429058)
XLA Ops:
  3.2 4.7 %collective-permute-start = (f32[2,16,16,1]{3,2,1,0:T(8,128)S(1)}, f32[2,16,16,1]{3,2,1,0:T(8,128)S(1)}, u32[]{:S(2)}, u32[]{:S(2)}) collective-permute-start(f32[2,16,16,1]{3,2,1,0:T(8,128)S(1)} %get-tuple-element.100), channel_id=1, source_target_pairs={{0,64},{64,128},{128,192},{192,256},{256,320},{320,384},{384,448},... | collective-permute-start | bytes 6152 | tf_op jit(solution)/shard_map/ppermute | solution.py:20
  9.5 6.2 %broadcast_multiply_fusion = (f32[16,16,128]{2,1,0:T(8,128)S(1)}, f32[16,16,128]{2,1,0:T(8,128)S(1)}, pred[16,16,128]{2,1,0:T(8,128)(4,1)S(1)}, pred[16,16,128]{...) fusion(f32[]{:T(128)} %bitcast.7, f32[]{:T(128)} %bitcast.6, ...), kind=kLoop, calls=%fused_computation.232 | loop fusion | flops 786432 | bytes 655392 | tf_op jit(solution)/shard_map/mul | solution.py:48
  18.5 8.7 %collective-permute-start.3 = (f32[2,16,1,130]{3,2,1,0:T(1,128)S(1)}, f32[2,16,1,130]{3,2,1,0:T(1,128)S(1)}, u32[]{:S(2)}, u32[]{:S(2)}) collective-permute-start(f32[2,16,1,130]{3,2,1,0:T(1,128)S(1)} %get-tuple-element.73), channel_id=1, source_target_pairs={{4,0},{8,4},{12,8},{16,12},{20,16},{24,20},{28,24},{32,28},{36,32}... | collective-permute-start | bytes 49928 | tf_op jit(solution)/shard_map/ppermute | solution.py:23
  29.2 6.2 %fusion.48 = (f32[1,16,16,128]{3,2,1,0:T(8,128)S(1)}, f32[16,16,128]{2,1,0:T(8,128)S(1)}, f32[16,16,128]{2,1,0:T(8,128)S(1)}) fusion(f32[2,16,16,128]{3,2,1,0:T(8,128)} %param.7, f32[16,16,128]{2,1,0:T(8,128)S(1)} %get-tuple-element.40, pred[16,16,128]{2,1,0:T(8,128)(4,1)S(1)} %get-tuple-element.48, f32[]{:T(128)} %bitcast.15, ...), kind=kLoop, calls=%fused_computation.163 | loop fusion | flops 786432 | bytes 1048608 | tf_op jit(solution)/shard_map/stack | solution.py:29
  37.5 4.0 %collective-permute-start.5 = (f32[2,1,18,130]{3,2,1,0:T(8,128)S(1)}, f32[2,1,18,130]{3,2,1,0:T(8,128)S(1)}, u32[]{:S(2)}, u32[]{:S(2)}) collective-permute-start(f32[2,1,18,130]{3,2,1,0:T(8,128)S(1)} %get-tuple-element.64), channel_id=1, source_target_pairs={{0,1},{1,2},{2,3},{4,5},{5,6},{6,7},{8,9},{9,10},{10,11},{12,13},{... | collective-permute-start | bytes 56168 | tf_op jit(solution)/shard_map/ppermute | solution.py:20
  47.8 4.0 %collective-permute-start.6 = (f32[2,16,16,1]{3,2,1,0:T(8,128)S(1)}, f32[2,16,16,1]{3,2,1,0:T(8,128)S(1)}, u32[]{:S(2)}, u32[]{:S(2)}) collective-permute-start(f32[2,16,16,1]{3,2,1,0:T(8,128)S(1)} %get-tuple-element.98), channel_id=1, source_target_pairs={{0,64},{64,128},{128,192},{192,256},{256,320},{320,384},{384,448},... | collective-permute-start | bytes 6152 | tf_op jit(solution)/shard_map/ppermute | solution.py:20
  55.8 4.7 %collective-permute-start.9 = (f32[2,16,1,130]{3,2,1,0:T(1,128)S(1)}, f32[2,16,1,130]{3,2,1,0:T(1,128)S(1)}, u32[]{:S(2)}, u32[]{:S(2)}) collective-permute-start(f32[2,16,1,130]{3,2,1,0:T(1,128)S(1)} %get-tuple-element.71), channel_id=1, source_target_pairs={{4,0},{8,4},{12,8},{16,12},{20,16},{24,20},{28,24},{32,28},{36,32}... | collective-permute-start | bytes 49928 | tf_op jit(solution)/shard_map/ppermute | solution.py:23
  65.0 4.3 %collective-permute-start.11 = (f32[2,1,18,130]{3,2,1,0:T(8,128)S(1)}, f32[2,1,18,130]{3,2,1,0:T(8,128)S(1)}, u32[]{:S(2)}, u32[]{:S(2)}) collective-permute-start(f32[2,1,18,130]{3,2,1,0:T(8,128)S(1)} %get-tuple-element.62), channel_id=1, source_target_pairs={{0,1},{1,2},{2,3},{4,5},{5,6},{6,7},{8,9},{9,10},{10,11},{12,13},{... | collective-permute-start | bytes 56168 | tf_op jit(solution)/shard_map/ppermute | solution.py:20
  74.6 4.8 %collective-permute-start.12 = (f32[2,16,16,1]{3,2,1,0:T(8,128)S(1)}, f32[2,16,16,1]{3,2,1,0:T(8,128)S(1)}, u32[]{:S(2)}, u32[]{:S(2)}) collective-permute-start(f32[2,16,16,1]{3,2,1,0:T(8,128)S(1)} %get-tuple-element.96), channel_id=1, source_target_pairs={{0,64},{64,128},{128,192},{192,256},{256,320},{320,384},{384,448},... | collective-permute-start | bytes 6152 | tf_op jit(solution)/shard_map/ppermute | solution.py:20
  93.1 4.6 %collective-permute-start.17 = (f32[2,1,18,130]{3,2,1,0:T(8,128)S(1)}, f32[2,1,18,130]{3,2,1,0:T(8,128)S(1)}, u32[]{:S(2)}, u32[]{:S(2)}) collective-permute-start(f32[2,1,18,130]{3,2,1,0:T(8,128)S(1)} %get-tuple-element.60), channel_id=1, source_target_pairs={{0,1},{1,2},{2,3},{4,5},{5,6},{6,7},{8,9},{9,10},{10,11},{12,13},{... | collective-permute-start | bytes 56168 | tf_op jit(solution)/shard_map/ppermute | solution.py:20
  101.4 4.8 %collective-permute-start.18 = (f32[2,16,16,1]{3,2,1,0:T(8,128)S(1)}, f32[2,16,16,1]{3,2,1,0:T(8,128)S(1)}, u32[]{:S(2)}, u32[]{:S(2)}) collective-permute-start(f32[2,16,16,1]{3,2,1,0:T(8,128)S(1)} %get-tuple-element.94), channel_id=1, source_target_pairs={{0,64},{64,128},{128,192},{192,256},{256,320},{320,384},{384,448},... | collective-permute-start | bytes 6152 | tf_op jit(solution)/shard_map/ppermute | solution.py:20
  106.1 4.6 %collective-permute-done.19 = f32[2,16,16,1]{3,2,1,0:T(8,128)S(1)} collective-permute-done((f32[2,16,16,1]{3,2,1,0:T(8,128)S(1)}, f32[2,16,16,1]{3,2,1,0:T(8,128)S(1)}, u32[]{:S(2)}, u32[]{:S(2)}) %collective-permute-start.19) | collective-permute-done | bytes 2080 | tf_op jit(solution)/shard_map/ppermute | solution.py:23
  118.1 9.7 %reshape.74 = f32[8,2,8,2,64,2]{5,4,3,2,1,0:T(8,128)} reshape(f32[16,16,128]{2,1,0:T(8,128)S(1)} %get-tuple-element.39) | data formatting | bytes 262144 | tf_op jit(solution)/shard_map/reshape | solution.py:72
  127.9 4.0 %reduce_sum.189 = f32[8,8,64]{2,1,0:T(8,128)S(1)} reduce(f32[8,2,8,2,64,2]{5,4,3,2,1,0:T(8,128)} %reshape.74, f32[]{:T(128)} %constant.19.clone.1), dimensions={1,3,5}, to_apply=%region_0.1 | reduce | flops 28672 | bytes 147460 | tf_op jit(solution)/shard_map/reduce_sum | solution.py:73
  133.3 4.5 %collective-permute-start.23 = (f32[2,1,18,130]{3,2,1,0:T(8,128)S(1)}, f32[2,1,18,130]{3,2,1,0:T(8,128)S(1)}, u32[]{:S(2)}, u32[]{:S(2)}) collective-permute-start(f32[2,1,18,130]{3,2,1,0:T(8,128)S(1)} %get-tuple-element.58), channel_id=1, source_target_pairs={{0,1},{1,2},{2,3},{4,5},{5,6},{6,7},{8,9},{9,10},{10,11},{12,13},{... | collective-permute-start | bytes 56168 | tf_op jit(solution)/shard_map/ppermute | solution.py:20
  140.2 18.0 %reshape.75 = f32[2,8,2,8,2,64,2]{6,5,4,3,2,1,0:T(8,128)} reshape(f32[2,16,16,128]{3,2,1,0:T(8,128)S(1)} %get-tuple-element.38) | data formatting | bytes 524288 | tf_op jit(solution)/shard_map/reshape | solution.py:72
  158.3 7.0 %reduce_sum.190 = f32[2,8,8,64]{3,2,1,0:T(8,128)S(1)} reduce(f32[2,8,2,8,2,64,2]{6,5,4,3,2,1,0:T(8,128)} %reshape.75, f32[]{:T(128)} %constant.19.clone.1), dimensions={2,4,6}, to_apply=%region_1.2 | reduce | flops 57344 | bytes 294916 | tf_op jit(solution)/shard_map/reduce_sum | solution.py:73
  166.7 4.7 %collective-permute-start.24 = (f32[2,8,8,1]{3,2,1,0:T(8,128)S(1)}, f32[2,8,8,1]{3,2,1,0:T(8,128)S(1)}, u32[]{:S(2)}, u32[]{:S(2)}) collective-permute-start(f32[2,8,8,1]{3,2,1,0:T(8,128)S(1)} %get-tuple-element.112), channel_id=1, source_target_pairs={{0,64},{64,128},{128,192},{192,256},{256,320},{320,384},{384,448},... | collective-permute-start | bytes 1544 | tf_op jit(solution)/shard_map/ppermute | solution.py:20
  172.9 3.9 %collective-permute-start.26 = (f32[2,8,1,66]{3,1,2,0:T(8,128)S(1)}, f32[2,8,1,66]{3,1,2,0:T(8,128)S(1)}, u32[]{:S(2)}, u32[]{:S(2)}) collective-permute-start(f32[2,8,1,66]{3,1,2,0:T(8,128)S(1)} %bitcast.257), channel_id=1, source_target_pairs={{0,4},{4,8},{8,12},{12,16},{16,20},{20,24},{24,28},{28,32},{32,36}... | collective-permute-start | bytes 12680 | tf_op jit(solution)/shard_map/ppermute | solution.py:20
  183.2 4.6 %collective-permute-start.29 = (f32[2,1,10,66]{3,2,1,0:T(8,128)S(1)}, f32[2,1,10,66]{3,2,1,0:T(8,128)S(1)}, u32[]{:S(2)}, u32[]{:S(2)}) collective-permute-start(f32[2,1,10,66]{3,2,1,0:T(8,128)S(1)} %get-tuple-element.102), channel_id=1, source_target_pairs={{0,1},{1,2},{2,3},{4,5},{5,6},{6,7},{8,9},{9,10},{10,11},{12,13},{... | collective-permute-start | bytes 15848 | tf_op jit(solution)/shard_map/ppermute | solution.py:20
  192.4 5.7 %collective-permute-start.30 = (f32[2,16,16,1]{3,2,1,0:T(8,128)S(1)}, f32[2,16,16,1]{3,2,1,0:T(8,128)S(1)}, u32[]{:S(2)}, u32[]{:S(2)}) collective-permute-start(f32[2,16,16,1]{3,2,1,0:T(8,128)S(1)} %get-tuple-element.92), channel_id=1, source_target_pairs={{0,64},{64,128},{128,192},{192,256},{256,320},{320,384},{384,448},... | collective-permute-start | bytes 6152 | tf_op jit(solution)/shard_map/ppermute | solution.py:20
  209.8 4.7 %collective-permute-start.32 = (f32[2,16,1,130]{3,2,1,0:T(1,128)S(1)}, f32[2,16,1,130]{3,2,1,0:T(1,128)S(1)}, u32[]{:S(2)}, u32[]{:S(2)}) collective-permute-start(f32[2,16,1,130]{3,2,1,0:T(1,128)S(1)} %get-tuple-element.66), channel_id=1, source_target_pairs={{0,4},{4,8},{8,12},{12,16},{16,20},{20,24},{24,28},{28,32},{32,36}... | collective-permute-start | bytes 49928 | tf_op jit(solution)/shard_map/ppermute | solution.py:20
  217.4 4.5 %collective-permute-start.35 = (f32[2,1,18,130]{3,2,1,0:T(8,128)S(1)}, f32[2,1,18,130]{3,2,1,0:T(8,128)S(1)}, u32[]{:S(2)}, u32[]{:S(2)}) collective-permute-start(f32[2,1,18,130]{3,2,1,0:T(8,128)S(1)} %get-tuple-element.56), channel_id=1, source_target_pairs={{0,1},{1,2},{2,3},{4,5},{5,6},{6,7},{8,9},{9,10},{10,11},{12,13},{... | collective-permute-start | bytes 56168 | tf_op jit(solution)/shard_map/ppermute | solution.py:20
  225.4 110.4 %all-reduce = (f32[2,8]{1,0:T(2,128)S(1)}, f32[1]{0:T(128)}, f32[1]{0:T(128)}, f32[1]{0:T(128)}) all-reduce(f32[2,8]{1,0:T(2,128)S(1)} %stack.254, f32[1]{0:T(128)} %bitcast.84, f32[1]{0:T(128)} %bitcast.81, f32[1]{0:T(128)} %bitcast.80), channel_id=1, replica_groups=mesh['gx'=8,'gy'=16,'gz'=4] {'gx','gy','gz'}, use_global_device_ids=true, to_apply=%region_18.19 | all-reduce | flops 19 | bytes 152 | tf_op jit(solution)/shard_map/psum | solution.py:118
  (141 shorter events, 94.2 us)
Async XLA Ops:
  1.9 15.4 %collective-permute-start.1 = (f32[2,16,16,1]{3,2,1,0:T(8,128)S(1)}, f32[2,16,16,1]{3,2,1,0:T(8,128)S(1)}, u32[]{:S(2)}, u32[]{:S(2)}) collective-permute-start(f32[2,16,16,1]{3,2,1,0:T(8,128)S(1)} %get-tuple-element.99), channel_id=1, source_target_pairs={{64,0},{128,64},{192,128},{256,192},{320,256},{384,320},{448,384},... | collective-permute-start | bytes 6152 | tf_op jit(solution)/shard_map/ppermute | solution.py:23
  3.2 14.1 %collective-permute-start = (f32[2,16,16,1]{3,2,1,0:T(8,128)S(1)}, f32[2,16,16,1]{3,2,1,0:T(8,128)S(1)}, u32[]{:S(2)}, u32[]{:S(2)}) collective-permute-start(f32[2,16,16,1]{3,2,1,0:T(8,128)S(1)} %get-tuple-element.100), channel_id=1, source_target_pairs={{0,64},{64,128},{128,192},{192,256},{256,320},{320,384},{384,448},... | collective-permute-start | bytes 6152 | tf_op jit(solution)/shard_map/ppermute | solution.py:20
  18.5 16.8 %collective-permute-start.3 = (f32[2,16,1,130]{3,2,1,0:T(1,128)S(1)}, f32[2,16,1,130]{3,2,1,0:T(1,128)S(1)}, u32[]{:S(2)}, u32[]{:S(2)}) collective-permute-start(f32[2,16,1,130]{3,2,1,0:T(1,128)S(1)} %get-tuple-element.73), channel_id=1, source_target_pairs={{4,0},{8,4},{12,8},{16,12},{20,16},{24,20},{28,24},{32,28},{36,32}... | collective-permute-start | bytes 49928 | tf_op jit(solution)/shard_map/ppermute | solution.py:23
  27.2 8.1 %collective-permute-start.2 = (f32[2,16,1,130]{3,2,1,0:T(1,128)S(1)}, f32[2,16,1,130]{3,2,1,0:T(1,128)S(1)}, u32[]{:S(2)}, u32[]{:S(2)}) collective-permute-start(f32[2,16,1,130]{3,2,1,0:T(1,128)S(1)} %get-tuple-element.74), channel_id=1, source_target_pairs={{0,4},{4,8},{8,12},{12,16},{16,20},{20,24},{24,28},{28,32},{32,36}... | collective-permute-start | bytes 49928 | tf_op jit(solution)/shard_map/ppermute | solution.py:20
  36.2 6.3 %collective-permute-start.4 = (f32[2,1,18,130]{3,2,1,0:T(8,128)S(1)}, f32[2,1,18,130]{3,2,1,0:T(8,128)S(1)}, u32[]{:S(2)}, u32[]{:S(2)}) collective-permute-start(f32[2,1,18,130]{3,2,1,0:T(8,128)S(1)} %get-tuple-element.63), channel_id=1, source_target_pairs={{1,0},{2,1},{3,2},{5,4},{6,5},{7,6},{9,8},{10,9},{11,10},{13,12},{... | collective-permute-start | bytes 56168 | tf_op jit(solution)/shard_map/ppermute | solution.py:23
  46.5 8.1 %collective-permute-start.7 = (f32[2,16,16,1]{3,2,1,0:T(8,128)S(1)}, f32[2,16,16,1]{3,2,1,0:T(8,128)S(1)}, u32[]{:S(2)}, u32[]{:S(2)}) collective-permute-start(f32[2,16,16,1]{3,2,1,0:T(8,128)S(1)} %get-tuple-element.97), channel_id=1, source_target_pairs={{64,0},{128,64},{192,128},{256,192},{320,256},{384,320},{448,384},... | collective-permute-start | bytes 6152 | tf_op jit(solution)/shard_map/ppermute | solution.py:23
  47.8 7.7 %collective-permute-start.6 = (f32[2,16,16,1]{3,2,1,0:T(8,128)S(1)}, f32[2,16,16,1]{3,2,1,0:T(8,128)S(1)}, u32[]{:S(2)}, u32[]{:S(2)}) collective-permute-start(f32[2,16,16,1]{3,2,1,0:T(8,128)S(1)} %get-tuple-element.98), channel_id=1, source_target_pairs={{0,64},{64,128},{128,192},{192,256},{256,320},{320,384},{384,448},... | collective-permute-start | bytes 6152 | tf_op jit(solution)/shard_map/ppermute | solution.py:20
  55.8 6.7 %collective-permute-start.9 = (f32[2,16,1,130]{3,2,1,0:T(1,128)S(1)}, f32[2,16,1,130]{3,2,1,0:T(1,128)S(1)}, u32[]{:S(2)}, u32[]{:S(2)}) collective-permute-start(f32[2,16,1,130]{3,2,1,0:T(1,128)S(1)} %get-tuple-element.71), channel_id=1, source_target_pairs={{4,0},{8,4},{12,8},{16,12},{20,16},{24,20},{28,24},{32,28},{36,32}... | collective-permute-start | bytes 49928 | tf_op jit(solution)/shard_map/ppermute | solution.py:23
  73.3 9.7 %collective-permute-start.13 = (f32[2,16,16,1]{3,2,1,0:T(8,128)S(1)}, f32[2,16,16,1]{3,2,1,0:T(8,128)S(1)}, u32[]{:S(2)}, u32[]{:S(2)}) collective-permute-start(f32[2,16,16,1]{3,2,1,0:T(8,128)S(1)} %get-tuple-element.95), channel_id=1, source_target_pairs={{64,0},{128,64},{192,128},{256,192},{320,256},{384,320},{448,384},... | collective-permute-start | bytes 6152 | tf_op jit(solution)/shard_map/ppermute | solution.py:23
  74.6 9.3 %collective-permute-start.12 = (f32[2,16,16,1]{3,2,1,0:T(8,128)S(1)}, f32[2,16,16,1]{3,2,1,0:T(8,128)S(1)}, u32[]{:S(2)}, u32[]{:S(2)}) collective-permute-start(f32[2,16,16,1]{3,2,1,0:T(8,128)S(1)} %get-tuple-element.96), channel_id=1, source_target_pairs={{0,64},{64,128},{128,192},{192,256},{256,320},{320,384},{384,448},... | collective-permute-start | bytes 6152 | tf_op jit(solution)/shard_map/ppermute | solution.py:20
  84.2 6.4 %collective-permute-start.15 = (f32[2,16,1,130]{3,2,1,0:T(1,128)S(1)}, f32[2,16,1,130]{3,2,1,0:T(1,128)S(1)}, u32[]{:S(2)}, u32[]{:S(2)}) collective-permute-start(f32[2,16,1,130]{3,2,1,0:T(1,128)S(1)} %get-tuple-element.69), channel_id=1, source_target_pairs={{4,0},{8,4},{12,8},{16,12},{20,16},{24,20},{28,24},{32,28},{36,32}... | collective-permute-start | bytes 49928 | tf_op jit(solution)/shard_map/ppermute | solution.py:23
  100.1 10.7 %collective-permute-start.19 = (f32[2,16,16,1]{3,2,1,0:T(8,128)S(1)}, f32[2,16,16,1]{3,2,1,0:T(8,128)S(1)}, u32[]{:S(2)}, u32[]{:S(2)}) collective-permute-start(f32[2,16,16,1]{3,2,1,0:T(8,128)S(1)} %get-tuple-element.93), channel_id=1, source_target_pairs={{64,0},{128,64},{192,128},{256,192},{320,256},{384,320},{448,384},... | collective-permute-start | bytes 6152 | tf_op jit(solution)/shard_map/ppermute | solution.py:23
  101.4 10.2 %collective-permute-start.18 = (f32[2,16,16,1]{3,2,1,0:T(8,128)S(1)}, f32[2,16,16,1]{3,2,1,0:T(8,128)S(1)}, u32[]{:S(2)}, u32[]{:S(2)}) collective-permute-start(f32[2,16,16,1]{3,2,1,0:T(8,128)S(1)} %get-tuple-element.94), channel_id=1, source_target_pairs={{0,64},{64,128},{128,192},{192,256},{256,320},{320,384},{384,448},... | collective-permute-start | bytes 6152 | tf_op jit(solution)/shard_map/ppermute | solution.py:20
  111.9 20.0 %collective-permute-start.21 = (f32[2,16,1,130]{3,2,1,0:T(1,128)S(1)}, f32[2,16,1,130]{3,2,1,0:T(1,128)S(1)}, u32[]{:S(2)}, u32[]{:S(2)}) collective-permute-start(f32[2,16,1,130]{3,2,1,0:T(1,128)S(1)} %get-tuple-element.67), channel_id=1, source_target_pairs={{4,0},{8,4},{12,8},{16,12},{20,16},{24,20},{28,24},{32,28},{36,32}... | collective-permute-start | bytes 49928 | tf_op jit(solution)/shard_map/ppermute | solution.py:23
  114.8 17.1 %collective-permute-start.20 = (f32[2,16,1,130]{3,2,1,0:T(1,128)S(1)}, f32[2,16,1,130]{3,2,1,0:T(1,128)S(1)}, u32[]{:S(2)}, u32[]{:S(2)}) collective-permute-start(f32[2,16,1,130]{3,2,1,0:T(1,128)S(1)} %get-tuple-element.68), channel_id=1, source_target_pairs={{0,4},{4,8},{8,12},{12,16},{16,20},{20,24},{24,28},{28,32},{32,36}... | collective-permute-start | bytes 49928 | tf_op jit(solution)/shard_map/ppermute | solution.py:20
  165.4 6.5 %collective-permute-start.25 = (f32[2,8,8,1]{3,2,1,0:T(8,128)S(1)}, f32[2,8,8,1]{3,2,1,0:T(8,128)S(1)}, u32[]{:S(2)}, u32[]{:S(2)}) collective-permute-start(f32[2,8,8,1]{3,2,1,0:T(8,128)S(1)} %get-tuple-element.111), channel_id=1, source_target_pairs={{64,0},{128,64},{192,128},{256,192},{320,256},{384,320},{448,384},... | collective-permute-start | bytes 1544 | tf_op jit(solution)/shard_map/ppermute | solution.py:23
  166.7 6.1 %collective-permute-start.24 = (f32[2,8,8,1]{3,2,1,0:T(8,128)S(1)}, f32[2,8,8,1]{3,2,1,0:T(8,128)S(1)}, u32[]{:S(2)}, u32[]{:S(2)}) collective-permute-start(f32[2,8,8,1]{3,2,1,0:T(8,128)S(1)} %get-tuple-element.112), channel_id=1, source_target_pairs={{0,64},{64,128},{128,192},{192,256},{256,320},{320,384},{384,448},... | collective-permute-start | bytes 1544 | tf_op jit(solution)/shard_map/ppermute | solution.py:20
  181.9 6.6 %collective-permute-start.28 = (f32[2,1,10,66]{3,2,1,0:T(8,128)S(1)}, f32[2,1,10,66]{3,2,1,0:T(8,128)S(1)}, u32[]{:S(2)}, u32[]{:S(2)}) collective-permute-start(f32[2,1,10,66]{3,2,1,0:T(8,128)S(1)} %get-tuple-element.101), channel_id=1, source_target_pairs={{1,0},{2,1},{3,2},{5,4},{6,5},{7,6},{9,8},{10,9},{11,10},{13,12},{... | collective-permute-start | bytes 15848 | tf_op jit(solution)/shard_map/ppermute | solution.py:23
  191.1 16.5 %collective-permute-start.31 = (f32[2,16,16,1]{3,2,1,0:T(8,128)S(1)}, f32[2,16,16,1]{3,2,1,0:T(8,128)S(1)}, u32[]{:S(2)}, u32[]{:S(2)}) collective-permute-start(f32[2,16,16,1]{3,2,1,0:T(8,128)S(1)} %get-tuple-element.91), channel_id=1, source_target_pairs={{64,0},{128,64},{192,128},{256,192},{320,256},{384,320},{448,384},... | collective-permute-start | bytes 6152 | tf_op jit(solution)/shard_map/ppermute | solution.py:23
  192.4 15.2 %collective-permute-start.30 = (f32[2,16,16,1]{3,2,1,0:T(8,128)S(1)}, f32[2,16,16,1]{3,2,1,0:T(8,128)S(1)}, u32[]{:S(2)}, u32[]{:S(2)}) collective-permute-start(f32[2,16,16,1]{3,2,1,0:T(8,128)S(1)} %get-tuple-element.92), channel_id=1, source_target_pairs={{0,64},{64,128},{128,192},{192,256},{256,320},{320,384},{384,448},... | collective-permute-start | bytes 6152 | tf_op jit(solution)/shard_map/ppermute | solution.py:20
  207.9 8.1 %collective-permute-start.33 = (f32[2,16,1,130]{3,2,1,0:T(1,128)S(1)}, f32[2,16,1,130]{3,2,1,0:T(1,128)S(1)}, u32[]{:S(2)}, u32[]{:S(2)}) collective-permute-start(f32[2,16,1,130]{3,2,1,0:T(1,128)S(1)} %get-tuple-element.65), channel_id=1, source_target_pairs={{4,0},{8,4},{12,8},{16,12},{20,16},{24,20},{28,24},{32,28},{36,32}... | collective-permute-start | bytes 49928 | tf_op jit(solution)/shard_map/ppermute | solution.py:23
  209.8 6.1 %collective-permute-start.32 = (f32[2,16,1,130]{3,2,1,0:T(1,128)S(1)}, f32[2,16,1,130]{3,2,1,0:T(1,128)S(1)}, u32[]{:S(2)}, u32[]{:S(2)}) collective-permute-start(f32[2,16,1,130]{3,2,1,0:T(1,128)S(1)} %get-tuple-element.66), channel_id=1, source_target_pairs={{0,4},{4,8},{8,12},{12,16},{16,20},{20,24},{24,28},{28,32},{32,36}... | collective-permute-start | bytes 49928 | tf_op jit(solution)/shard_map/ppermute | solution.py:20
  216.1 8.1 %collective-permute-start.34 = (f32[2,1,18,130]{3,2,1,0:T(8,128)S(1)}, f32[2,1,18,130]{3,2,1,0:T(8,128)S(1)}, u32[]{:S(2)}, u32[]{:S(2)}) collective-permute-start(f32[2,1,18,130]{3,2,1,0:T(8,128)S(1)} %get-tuple-element.55), channel_id=1, source_target_pairs={{1,0},{2,1},{3,2},{5,4},{6,5},{7,6},{9,8},{10,9},{11,10},{13,12},{... | collective-permute-start | bytes 56168 | tf_op jit(solution)/shard_map/ppermute | solution.py:23
  217.4 6.8 %collective-permute-start.35 = (f32[2,1,18,130]{3,2,1,0:T(8,128)S(1)}, f32[2,1,18,130]{3,2,1,0:T(8,128)S(1)}, u32[]{:S(2)}, u32[]{:S(2)}) collective-permute-start(f32[2,1,18,130]{3,2,1,0:T(8,128)S(1)} %get-tuple-element.56), channel_id=1, source_target_pairs={{0,1},{1,2},{2,3},{4,5},{5,6},{6,7},{8,9},{9,10},{10,11},{12,13},{... | collective-permute-start | bytes 56168 | tf_op jit(solution)/shard_map/ppermute | solution.py:20
  (19 other events, 517.3 us)
where the time goes:
time: 341 us; the launch traced here: 339 us
  starting transfers between devices  113 us (33%)
  blocking collectives  110 us (32%)
  other arithmetic  55.5 us (16%)
  local copies, waits for them, and re-layouts  34.4 us (10%)
  waiting for transfers between devices  24.1 us (7%)
    psum x1, blocking collectives, shards(): fin_sq, grad_sums = lax.psum((fin_sq, grad_sums), ('gx', 'gy', 'gz'))  110 us
    ppermute x18, starting transfers between devices, extended(): lax.ppermute(lax.slice_in_dim(block, block.shape[dim] - width, None, axis...  73.4 us
    ppermute x18, starting transfers between devices, extended(): lax.ppermute(lax.slice_in_dim(block, 0, width, axis=dim), axis, backward)  39.5 us
    reshape x2, local copies, waits for them, and re-layouts, restrict(): blocks = field.reshape(lead + (zlen // 2, 2, ylen // 2, 2, xlen // 2, 2))  27.8 us
    ppermute x18, waiting for transfers between devices, extended(): lax.ppermute(lax.slice_in_dim(block, 0, width, axis=dim), axis, backward)  14.6 us
    reduce_sum x2, other arithmetic, restrict(): return jnp.mean(blocks, axis=(-5, -3, -1))  11 us
    another operation x8, other arithmetic, shards(): grad_sums = jnp.stack(sums, axis=1)  10.6 us
    ppermute x18, waiting for transfers between devices, extended(): lax.ppermute(lax.slice_in_dim(block, block.shape[dim] - width, None, axis...  9.54 us
  transfers between devices with their start and end apart: 36, of which 16 were waited for; matrix products, arithmetic and copies ran while one was open for 13% of the time, Pallas kernels for 0%

commit v1 on v0

v1 whole, which is shorter than its diff:
```python
import functools

import jax
import jax.numpy as jnp
from jax import lax
from jax.experimental import pallas as pl
from jax.experimental.pallas import tpu as pltpu
from jax.sharding import PartitionSpec as P

MESH = pl.DeviceIdType.MESH
NMAT = 8
KH2 = 0.5
SHIFT = 0.5
F32 = jnp.float32
AXES = ("gx", "gy", "gz")


def near_offsets():
    return [
        (dx, dy, dz)
        for dx in (-1, 0, 1)
        for dy in (-1, 0, 1)
        for dz in (-1, 0, 1)
        if (dx, dy, dz) != (0, 0, 0)
    ]


def kernel(
    sizes,
    guess_hbm,
    source_hbm,
    forward_hbm,
    labels_hbm,
    pr_ref,
    pi_ref,
    adj_hbm,
    row_ref,
    F,
    B,
    H,
    D,
    FW,
    LI,
    RP,
    E,
    E1,
    G,
    ADJ,
    ER,
    TB,
    PU,
    PL,
    PG,
    PE,
    RU,
    RL,
    RG,
    RE,
    ACC,
    VAL,
    R1,
    R2,
    local_sem,
    send_a,
    recv_a,
    send_c,
    recv_c,
    send_r,
    recv_r,
):
    nx, ny, nz = sizes
    gx, gy, gz = (lax.axis_index(a) for a in AXES)

    def device(offset):
        dx, dy, dz = offset
        return {
            "gx": lax.rem(gx + (dx % nx), nx),
            "gy": lax.rem(gy + (dy % ny), ny),
            "gz": lax.rem(gz + (dz % nz), nz),
        }

    loads = [
        pltpu.make_async_copy(labels_hbm, LI, local_sem.at[0]),
        pltpu.make_async_copy(guess_hbm, F.at[0:2, 0, pl.ds(4, 16), pl.ds(8, 16)], local_sem.at[1]),
        pltpu.make_async_copy(source_hbm, F.at[2:4, 0, pl.ds(4, 16), pl.ds(8, 16)], local_sem.at[2]),
        pltpu.make_async_copy(forward_hbm, FW, local_sem.at[3]),
    ]
    for copy in loads:
        copy.start()

    y_peers = [(0, dy, 0) for dy in range(1, ny)]
    xz_peers = [(dx, 0, dz) for dx in range(nx) for dz in range(nz) if (dx, dz) != (0, 0)]
    met = {(dx % nx, dy % ny, dz % nz) for dx, dy, dz in near_offsets() + y_peers + xz_peers}
    barrier = pltpu.get_barrier_semaphore()
    for offset in sorted(met):
        pl.semaphore_signal(barrier, inc=1, device_id=device(offset), device_id_type=MESH)

    lane = lax.broadcasted_iota(jnp.int32, (8, 128), 1)
    row8 = lax.broadcasted_iota(jnp.int32, (8, 128), 0)
    even_lane = lane % 2 == 0
    even_row = row8 % 2 == 0
    left_half = lane % 8 < 4
    slot_of = lane // 8
    left_ok = (gx > 0).astype(F32)
    right_ok = (gx < nx - 1).astype(F32)
    side_ok = jnp.where(lane < 64, right_ok, left_ok)
    slot_ok = jnp.where(left_half, left_ok, right_ok)

    for m in range(NMAT):
        er = jnp.full((8, 128), pr_ref[m], F32)
        ei = jnp.full((8, 128), pi_ref[m], F32)
        dr = 6.0 - KH2 * (er + SHIFT * ei)
        di = -KH2 * (SHIFT * er - ei)
        half = 0.5 / (dr * dr + di * di)
        TB[0, m] = dr * half
        TB[1, m] = -di * half
        TB[2, m] = dr
        TB[3, m] = di
        TB[4, m] = er

    def look_up(label, tables):
        high = label >= 3.5
        rest = jnp.where(high, label - 4.0, label)
        middle = rest >= 1.5
        odd = jnp.where(middle, rest - 2.0, rest) >= 0.5
        out = []
        for t in tables:
            pairs = [jnp.where(odd, TB[t, 2 * i + 1], TB[t, 2 * i]) for i in range(4)]
            quads = [jnp.where(middle, pairs[2 * i + 1], pairs[2 * i]) for i in range(2)]
            out.append(jnp.where(high, quads[1], quads[0]))
        return out

    def block_sum(v):
        v = v + jnp.where(even_row, pltpu.roll(v, 7, 0), pltpu.roll(v, 1, 0))
        return v + jnp.where(even_lane, pltpu.roll(v, 127, 1), pltpu.roll(v, 1, 1))

    loads[0].wait()

    def own_coefficients(z, carry):
        for yh in range(2):
            label = LI[z, 8 * yh : 8 * yh + 8].astype(F32)
            F[4, 0, z + 4, 8 + 8 * yh : 16 + 8 * yh] = label
            hr, hi, dr, di, er = look_up(label, (0, 1, 2, 3, 4))
            H[0, 0, z + 4, 8 + 8 * yh : 16 + 8 * yh] = hr
            H[1, 0, z + 4, 8 + 8 * yh : 16 + 8 * yh] = hi
            D[0, z, 8 * yh : 8 * yh + 8] = dr
            D[1, z, 8 * yh : 8 * yh + 8] = di
            ER[z, 8 * yh : 8 * yh + 8] = er
        return carry

    lax.fori_loop(0, 16, own_coefficients, 0)

    def own_coarse(zc, carry):
        for yh in range(2):
            rows = slice(8 * yh, 8 * yh + 8)
            q4 = (KH2 * 4.0 / 8.0) * block_sum(ER[2 * zc, rows] + ER[2 * zc + 1, rows])
            scale = 0.5 / (36.0 + q4 * q4)
            G[0, 0, zc + 2, 8 + 8 * yh : 16 + 8 * yh] = 6.0 * scale
            G[1, 0, zc + 2, 8 + 8 * yh : 16 + 8 * yh] = -q4 * scale
        return carry

    lax.fori_loop(0, 8, own_coarse, 0)

    def pack(pieces):
        total = jnp.zeros((8, 128), F32)
        for slot, piece in enumerate(pieces):
            total = jnp.where(slot_of == slot, pltpu.roll(piece, (8 * slot + 4) % 128, 1), total)
        return total

    for yh in range(2):
        rows = slice(8 + 8 * yh, 16 + 8 * yh)
        PL[yh] = pack([F[4, 0, 4 + z, rows] for z in range(16)])
        PG[yh] = pack([G[c, 0, 2 + z, rows] for c in range(2) for z in range(8)])
    loads[1].wait()
    loads[2].wait()

    def pack_quarter(zq, carry):
        for yh in range(2):
            rows = slice(8 + 8 * yh, 16 + 8 * yh)
            PU[zq, yh] = pack([F[f, 0, 4 + 4 * zq + p, rows] for f in range(4) for p in range(4)])
        return carry

    lax.fori_loop(0, 4, pack_quarter, 0)

    def planes(dz, own, deep, at):
        if dz == 0:
            return pl.ds(at, own), pl.ds(at, own)
        if dz > 0:
            return pl.ds(at + own - deep, deep), pl.ds(at - deep, deep)
        return pl.ds(at, deep), pl.ds(at + own, deep)

    started = []

    def send(offset, source, target, sends, receives):
        k = len(started)
        copy = pltpu.make_async_remote_copy(
            src_ref=source,
            dst_ref=target,
            send_sem=sends.at[k],
            recv_sem=receives.at[k],
            device_id=device(offset),
            device_id_type=MESH,
        )
        copy.start()
        started.append(copy)

    pl.semaphore_wait(barrier, len(met))

    for offset in near_offsets():
        dx, dy, dz = offset
        if dx == 0:
            from_z, to_z = planes(dz, 16, 4, 4)
            from_y, to_y = planes(dy, 16, 4, 8)
            send(offset, F.at[:, 0, from_z, from_y], F.at[:, 0, to_z, to_y], send_a, recv_a)
        else:
            side = 0 if dx > 0 else 1
            from_z, to_z = planes(dz, 4, 1, 1)
            from_y, to_y = planes(dy, 2, 1, 1)
            from_z = pl.ds(from_z.start - 1, from_z.size)
            from_y = pl.ds(from_y.start - 1, from_y.size)
            send(offset, PU.at[from_z, from_y], RU.at[side, to_z, to_y], send_a, recv_a)
            send(offset, PL.at[from_y], RL.at[side, 1 - dz, to_y], send_a, recv_a)
    for offset in ((0, 0, 1), (0, 0, -1), (0, 1, 0), (0, -1, 0)):
        from_z, to_z = planes(offset[2], 8, 1, 2)
        from_y, to_y = planes(offset[1], 16, 4, 8)
        send(offset, G.at[:, 0, from_z, from_y], G.at[:, 0, to_z, to_y], send_a, recv_a)
    for offset in ((1, 0, 0), (-1, 0, 0)):
        send(offset, PG, RG.at[0 if offset[0] > 0 else 1], send_a, recv_a)

    for copy in started:
        copy.wait()
    loads[3].wait()

    def merged(low, high):
        return jnp.where(left_half, low, high) * slot_ok

    def unpack_quarter(zq, carry):
        for yg in range(4):
            both = merged(RU[0, zq, yg], RU[1, zq, yg])
            for f in range(4):
                for p in range(4):
                    slot = 4 * f + p
                    F[f, 1, 4 * zq + p, 8 * yg : 8 * yg + 8] = pltpu.roll(both, (124 - 8 * slot) % 128, 1)
        return carry

    lax.fori_loop(0, 6, unpack_quarter, 0)

    y_ok = [(gy > 0).astype(F32), 1.0, 1.0, (gy < ny - 1).astype(F32)]

    def halo_coefficients(z, carry):
        z_ok = ((z >= 4) | (gz > 0)).astype(F32) * ((z < 20) | (gz < nz - 1)).astype(F32)
        part = (z + 12) // 16
        shift = 124 - 8 * lax.rem(z + 12, 16)
        for yg in range(4):
            rows = slice(8 * yg, 8 * yg + 8)
            label = pltpu.roll(merged(RL[0, part, yg], RL[1, part, yg]), shift, 1)
            hr, hi = look_up(label, (0, 1))
            ok = side_ok * (z_ok * y_ok[yg])
            H[0, 1, z, rows] = hr * ok
            H[1, 1, z, rows] = hi * ok
        for yg in (0, 3):
            rows = slice(8 * yg, 8 * yg + 8)
            hr, hi = look_up(F[4, 0, z, rows], (0, 1))
            ok = z_ok * y_ok[yg]
            H[0, 0, z, rows] = hr * ok
            H[1, 0, z, rows] = hi * ok
        return carry

    lax.fori_loop(1, 23, halo_coefficients, 0)

    def halo_planes(z, carry):
        low_ok, high_ok = (gz > 0).astype(F32), (gz < nz - 1).astype(F32)
        for at, ok in ((z, low_ok), (z + 19, high_ok)):
            for yg in (1, 2):
                rows = slice(8 * yg, 8 * yg + 8)
                hr, hi = look_up(F[4, 0, at, rows], (0, 1))
                H[0, 0, at, rows] = hr * ok
                H[1, 0, at, rows] = hi * ok
        return carry

    lax.fori_loop(1, 4, halo_planes, 0)

    @pl.when(gz == 0)
    def _():
        F[0:2, :, 0:4] = jnp.zeros((2, 2, 4, 32, 128), F32)
        G[:, 0, 1] = jnp.zeros((2, 32, 128), F32)

    @pl.when(gz == nz - 1)
    def _():
        F[0:2, :, 20:24] = jnp.zeros((2, 2, 4, 32, 128), F32)
        G[:, 0, 10] = jnp.zeros((2, 32, 128), F32)

    @pl.when(gy == 0)
    def _():
        F[0:2, :, :, 0:8] = jnp.zeros((2, 2, 24, 8, 128), F32)
        G[:, 0, :, 0:8] = jnp.zeros((2, 12, 8, 128), F32)

    @pl.when(gy == ny - 1)
    def _():
        F[0:2, :, :, 24:32] = jnp.zeros((2, 2, 24, 8, 128), F32)
        G[:, 0, :, 24:32] = jnp.zeros((2, 12, 8, 128), F32)

    for yh in range(2):
        both = merged(RG[0, yh], RG[1, yh])
        for c in range(2):
            for z in range(8):
                G[c, 1, 2 + z, 8 + 8 * yh : 16 + 8 * yh] = pltpu.roll(both, (124 - 8 * (8 * c + z)) % 128, 1)

    def across(main, ext, step, tiles):
        at = lax.broadcasted_iota(jnp.int32, main.shape, 1)
        low, high = at < step, at >= 128 - step
        ml, el = pltpu.roll(main, step, 1), pltpu.roll(ext, step, 1)
        mr, er = pltpu.roll(main, 128 - step, 1), pltpu.roll(ext, 128 - step, 1)
        out = [jnp.where(low, el, ml) + jnp.where(high, er, mr)]
        if tiles == 2:
            out.append(jnp.where(low, ml, el) + jnp.where(high, mr, er))
        return out

    def sweep(source, target, first, last):
        def plane(z, carry):
            for rows in (4, 12, 20):
                mid = pl.ds(rows, 8)
                near = [[None, None], [None, None]]
                centre = [[None, None], [None, None]]
                for c in range(2):
                    main, ext = source[c, 0, z, mid], source[c, 1, z, mid]
                    centre[c] = [main, ext]
                    side = across(main, ext, 1, 2)
                    for t in range(2):
                        near[c][t] = (
                            side[t]
                            + (source[c, t, z - 1, mid] + source[c, t, z + 1, mid])
                            + (source[c, t, z, pl.ds(rows - 1, 8)] + source[c, t, z, pl.ds(rows + 1, 8)])
                        )
                for t in range(2):
                    wr = F[2, t, z, mid] + near[0][t]
                    wi = F[3, t, z, mid] + near[1][t]
                    hr, hi = H[0, t, z, mid], H[1, t, z, mid]
                    target[0, t, z, mid] = 0.5 * centre[0][t] + (hr * wr - hi * wi)
                    target[1, t, z, mid] = 0.5 * centre[1][t] + (hr * wi + hi * wr)
            return carry

        lax.fori_loop(first, last, plane, 0)

    sweep(F, B, 1, 23)
    sweep(B, F, 2, 22)
    sweep(F, B, 3, 21)

    zero = jnp.zeros((8, 128), F32)

    def residual(zc, carry):
        src_sq, pre_sq = carry
        for yh in range(2):
            rows = 8 + 8 * yh
            mid, out = pl.ds(rows, 8), slice(8 * yh, 8 * yh + 8)
            sums = [zero, zero]
            for k in range(2):
                z = 2 * zc + k
                near, centre = [], []
                for c in range(2):
                    main = B[c, 0, z + 4, mid]
                    centre.append(main)
                    side = across(main, B[c, 1, z + 4, mid], 1, 1)[0]
                    near.append(
                        side
                        + (B[c, 0, z + 3, mid] + B[c, 0, z + 5, mid])
                        + (B[c, 0, z + 4, pl.ds(rows - 1, 8)] + B[c, 0, z + 4, pl.ds(rows + 1, 8)])
                    )
                dr, di = D[0, z, out], D[1, z, out]
                sr, si = F[2, 0, z + 4, mid], F[3, 0, z + 4, mid]
                rr = sr + near[0] - (dr * centre[0] - di * centre[1])
                ri = si + near[1] - (dr * centre[1] + di * centre[0])
                RP[0, z, out] = rr
                RP[1, z, out] = ri
                src_sq = src_sq + (sr * sr + si * si)
                pre_sq = pre_sq + (rr * rr + ri * ri)
                sums = [sums[0] + rr, sums[1] + ri]
            br, bi = 0.5 * block_sum(sums[0]), 0.5 * block_sum(sums[1])
            wr, wi = G[0, 0, zc + 2, mid], G[1, 0, zc + 2, mid]
            E[0, 0, zc + 2, mid] = wr * br - wi * bi
            E[1, 0, zc + 2, mid] = wr * bi + wi * br
        return src_sq, pre_sq

    src_sq, pre_sq = lax.fori_loop(0, 8, residual, (zero, zero))

    for yh in range(2):
        PE[yh] = pack([E[c, 0, 2 + z, 8 + 8 * yh : 16 + 8 * yh] for c in range(2) for z in range(8)])
    del started[:]
    for offset in near_offsets():
        dx, dy, dz = offset
        if dx and dy and dz:
            continue
        if dx == 0:
            from_z, to_z = planes(dz, 8, 1 if dy else 2, 2)
            from_y, to_y = planes(dy, 16, 4, 8)
            send(offset, E.at[:, 0, from_z, from_y], E.at[:, 0, to_z, to_y], send_c, recv_c)
        else:
            side = 0 if dx > 0 else 1
            from_y, to_y = planes(dy, 2, 1, 1)
            from_y = pl.ds(from_y.start - 1, from_y.size)
            send(offset, PE.at[from_y], RE.at[side, 1 - dz, to_y], send_c, recv_c)
    for copy in started:
        copy.wait()

    for part, where in ((1, range(8)), (0, (7,)), (2, (0,))):
        for yg in range(4) if part == 1 else (1, 2):
            both = merged(RE[0, part, yg], RE[1, part, yg])
            for c in range(2):
                for z in where:
                    at = 2 + z if part == 1 else (1 if part == 0 else 10)
                    E[c, 1, at, 8 * yg : 8 * yg + 8] = pltpu.roll(both, (124 - 8 * (8 * c + z)) % 128, 1)

    @pl.when(gz == 0)
    def _():
        E[:, :, 0:2] = jnp.zeros((2, 2, 2, 32, 128), F32)

    @pl.when(gz == nz - 1)
    def _():
        E[:, :, 10:12] = jnp.zeros((2, 2, 2, 32, 128), F32)

    @pl.when(gy == 0)
    def _():
        E[:, :, :, 0:8] = jnp.zeros((2, 2, 12, 8, 128), F32)

    @pl.when(gy == ny - 1)
    def _():
        E[:, :, :, 24:32] = jnp.zeros((2, 2, 12, 8, 128), F32)

    def coarse(zc, row_groups, tiles):
        for rows in row_groups:
            mid = pl.ds(rows, 8)
            near, centre = [], []
            for c in range(2):
                main, ext = E[c, 0, zc, mid], E[c, 1, zc, mid]
                side = across(main, ext, 2, tiles)
                centre.append([main, ext])
                near.append(
                    [
                        side[t]
                        + (E[c, t, zc - 1, mid] + E[c, t, zc + 1, mid])
                        + (E[c, t, zc, pl.ds(rows - 2, 8)] + E[c, t, zc, pl.ds(rows + 2, 8)])
                        for t in range(tiles)
                    ]
                )
            for t in range(tiles):
                wr, wi = G[0, t, zc, mid], G[1, t, zc, mid]
                E1[0, t, zc, mid] = 1.5 * centre[0][t] + (wr * near[0][t] - wi * near[1][t])
                E1[1, t, zc, mid] = 1.5 * centre[1][t] + (wr * near[1][t] + wi * near[0][t])

    def own_planes(zc, carry):
        coarse(zc, (8, 16), 2)
        coarse(zc, (4, 20), 1)
        return carry

    lax.fori_loop(2, 10, own_planes, 0)
    coarse(1, (8, 16), 1)
    coarse(10, (8, 16), 1)

    def correct(zc, carry):
        carry = list(carry)
        for yh in range(2):
            rows = 8 + 8 * yh
            mid, out = pl.ds(rows, 8), slice(8 * yh, 8 * yh + 8)
            e, base = [], []
            for c in range(2):
                main = E1[c, 0, zc + 2, mid]
                side = across(main, E1[c, 1, zc + 2, mid], 1, 1)[0]
                e.append(main)
                base.append(
                    main + side + (E1[c, 0, zc + 2, pl.ds(rows - 1, 8)] + E1[c, 0, zc + 2, pl.ds(rows + 1, 8)])
                )
            for k in range(2):
                z = 2 * zc + k
                dr, di = D[0, z, out], D[1, z, out]
                rr = RP[0, z, out] + (base[0] + E1[0, 0, zc + 1 + 2 * k, mid]) - (dr * e[0] - di * e[1])
                ri = RP[1, z, out] + (base[1] + E1[1, 0, zc + 1 + 2 * k, mid]) - (dr * e[1] + di * e[0])
                carry[0] = carry[0] + (rr * rr + ri * ri)
                ar = B[0, 0, z + 4, mid] + e[0]
                ai = B[1, 0, z + 4, mid] + e[1]
                ADJ[0, z, out] = ar
                ADJ[1, z, out] = ai
                fr, fi = FW[0, z, out], FW[1, z, out]
                pr = fr * ar - fi * ai
                pi = fr * ai + fi * ar
                label = LI[z, out]
                for m in range(NMAT):
                    chosen = label == m
                    carry[1 + m] = carry[1 + m] + jnp.where(chosen, pr, 0.0)
                    carry[9 + m] = carry[9 + m] + jnp.where(chosen, pi, 0.0)
        return tuple(carry)

    sums = lax.fori_loop(0, 8, correct, (zero,) * 17)
    store = pltpu.make_async_copy(ADJ, adj_hbm, local_sem.at[0])
    store.start()

    ordered = list(sums[1:]) + [src_sq, pre_sq, sums[0]]
    ACC[...] = jnp.zeros((24, 128), F32)
    for k, value in enumerate(ordered):
        ACC[k : k + 1] = jnp.sum(value, axis=0, keepdims=True)
    totals = jnp.sum(ACC[...], axis=1, keepdims=True)
    lane24 = lax.broadcasted_iota(jnp.int32, (24, 128), 1)
    row24 = lax.broadcasted_iota(jnp.int32, (24, 128), 0)
    row = jnp.sum(jnp.where(lane24 == row24, totals, 0.0), axis=0, keepdims=True)

    for stage, (peers, slots, own) in enumerate(((y_peers, R1, gy), (xz_peers, R2, gx * nz + gz))):
        count = len(peers)
        VAL[stage] = row
        for offset in peers:
            pltpu.make_async_remote_copy(
                src_ref=VAL.at[stage],
                dst_ref=slots.at[own],
                send_sem=send_r.at[stage],
                recv_sem=recv_r.at[stage],
                device_id=device(offset),
                device_id_type=MESH,
            ).start()
        slots[own] = row
        every = pltpu.make_async_remote_copy(
            src_ref=slots.at[pl.ds(0, count)],
            dst_ref=slots.at[pl.ds(0, count)],
            send_sem=send_r.at[stage],
            recv_sem=recv_r.at[stage],
            device_id=device(peers[0]),
            device_id_type=MESH,
        )
        every.wait_recv()
        every.wait_send()
        row = slots[0]
        for k in range(1, count + 1):
            row = row + slots[k]

    cells = float(nx * ny * nz * 16 * 16 * 128)
    one = lax.broadcasted_iota(jnp.int32, (1, 128), 1)
    row_ref[...] = jnp.where(one < 2 * NMAT, (-KH2 / cells**0.5) * row, jnp.sqrt(jnp.maximum(row, 0.0) / cells))
    store.wait()


def shards(sizes, source, adjoint_guess, forward_field, labels, perm_real, perm_imag):
    vmem = lambda *shape: pltpu.VMEM(shape, F32)
    dma = pltpu.SemaphoreType.DMA
    n_a, n_c = 50, 18
    adjoint, row = pl.pallas_call(
        functools.partial(kernel, sizes),
        out_shape=(
            jax.ShapeDtypeStruct(adjoint_guess.shape, F32),
            jax.ShapeDtypeStruct((1, 128), F32),
        ),
        in_specs=[pl.BlockSpec(memory_space=pl.ANY)] * 4 + [pl.BlockSpec(memory_space=pltpu.SMEM)] * 2,
        out_specs=(pl.BlockSpec(memory_space=pl.ANY), pl.BlockSpec(memory_space=pltpu.VMEM)),
        scratch_shapes=[
            vmem(5, 2, 24, 32, 128),
            vmem(2, 2, 24, 32, 128),
            vmem(2, 2, 24, 32, 128),
            vmem(2, 16, 16, 128),
            vmem(2, 16, 16, 128),
            pltpu.VMEM((16, 16, 128), jnp.int32),
            vmem(2, 16, 16, 128),
            vmem(2, 2, 12, 32, 128),
            vmem(2, 2, 12, 32, 128),
            vmem(2, 2, 12, 32, 128),
            vmem(2, 16, 16, 128),
            vmem(16, 16, 128),
            vmem(5, 8, 8, 128),
            vmem(4, 2, 8, 128),
            vmem(2, 8, 128),
            vmem(2, 8, 128),
            vmem(2, 8, 128),
            vmem(2, 6, 4, 8, 128),
            vmem(2, 3, 4, 8, 128),
            vmem(2, 2, 8, 128),
            vmem(2, 3, 4, 8, 128),
            vmem(24, 128),
            vmem(2, 1, 128),
            vmem(sizes[1], 1, 128),
            vmem(sizes[0] * sizes[2], 1, 128),
            dma((4,)),
            dma((n_a,)),
            dma((n_a,)),
            dma((n_c,)),
            dma((n_c,)),
            dma((2,)),
            dma((2,)),
        ],
        compiler_params=pltpu.CompilerParams(collective_id=0, has_side_effects=True, vmem_limit_bytes=40 << 20),
    )(adjoint_guess, source, forward_field, labels, perm_real, perm_imag)
    material_grad = row[0, : 2 * NMAT].reshape(2, NMAT)
    norms = row[0, 2 * NMAT : 2 * NMAT + 3]
    return adjoint, material_grad, norms


def solution(mesh):
    sizes = tuple(mesh.shape[a] for a in AXES)
    field = P(None, "gz", "gy", "gx")
    return jax.shard_map(
        functools.partial(shards, sizes),
        mesh=mesh,
        in_specs=(field, field, field, P("gz", "gy", "gx"), P(), P()),
        out_specs=(field, P(), P()),
        check_vma=False,
    )
```

time: 341 us -> 61.5 us (0.18)
  starting transfers between devices: 113 us -> 0 us
  blocking collectives: 110 us -> 0 us
  other arithmetic: 55.5 us -> 0 us
  Pallas kernels: 0 us -> 53.6 us
  local copies, waits for them, and re-layouts: 34.4 us -> 7 us
  waiting for transfers between devices: 24.1 us -> 0 us
    ppermute x36 -> x0, starting transfers between devices: 113 us -> none  [the longest x18 73.4 us: extended(): lax.ppermute(lax.slice_in_dim(block, block.shape[dim] - width, None, axis...]
    psum x1 -> x0, blocking collectives: 110 us -> none  [shards(): fin_sq, grad_sums = lax.psum((fin_sq, grad_sums), ('gx', 'gy', 'gz'))]
    pallas_call x0 -> x1, Pallas kernels: none -> 53.6 us  [shards(): pl.pallas_call(functools.partial(kernel, sizes), out_shape=(jax.ShapeDtyp...]
    reshape x3 -> x0, local copies, waits for them, and re-layouts: 28.1 us -> none  [the longest x2 27.8 us: restrict(): blocks = field.reshape(lead + (zlen // 2, 2, ylen // 2, 2, xlen // 2, 2))]
    ppermute x36 -> x0, waiting for transfers between devices: 24.1 us -> none  [the longest x18 14.6 us: extended(): lax.ppermute(lax.slice_in_dim(block, 0, width, axis=dim), axis, backward)]
    another operation x18 -> x0, other arithmetic: 19.1 us -> none  [the longest x8 10.6 us: shards(): grad_sums = jnp.stack(sums, axis=1)]
    reduce_sum x6 -> x0, other arithmetic: 16 us -> none  [the longest x2 11 us: restrict(): return jnp.mean(blocks, axis=(-5, -3, -1))]
    mul x4 -> x0, other arithmetic: 6.74 us -> none  [the longest x1 6.15 us: coefficients(): shift_im = KH2 * (SHIFT * eps_re - eps_im)]
  transfers between devices with their start and end apart: 36 -> 0, of which waited for: 16 -> 0; matrix products, arithmetic and copies ran while one was open for 13% -> 0% of each run, Pallas kernels for 0% -> 0%
where the time goes in v1:
time: 61.5 us; the launch traced here: 61.3 us
  Pallas kernels  53.6 us (87%)
  local copies, waits for them, and re-layouts  7 us (11%)
  between operations  0.66 us (1%)
    pallas_call x1, Pallas kernels, shards(): pl.pallas_call(functools.partial(kernel, sizes), out_shape=(jax.ShapeDtyp...  53.6 us
    unnamed x13, local copies, waits for them, and re-layouts  5.76 us

profile of v1, /device:TPU:1, one launch (start us, length us, event | category | flops | bytes accessed | tf_op | source)
XLA Modules:
  0.0 61.3 jit_solution(3718569660043886258)
XLA Ops:
  0.6 0.0 copy-start
  0.6 0.9 %copy-done = f32[2,16,16,128]{3,2,1,0:T(8,128)S(1)} copy-done((f32[2,16,16,128]{3,2,1,0:T(8,128)S(1)}, f32[2,16,16,128]{3,2,1,0:T(8,128)}, u32[]{:S(2)}) %copy-start) | copy-done | bytes 262168
  1.6 0.0 copy-start.1
  1.6 0.9 %copy-done.1 = f32[2,16,16,128]{3,2,1,0:T(8,128)S(1)} copy-done((f32[2,16,16,128]{3,2,1,0:T(8,128)S(1)}, f32[2,16,16,128]{3,2,1,0:T(8,128)}, u32[]{:S(2)}) %copy-start.1) | copy-done | bytes 262168
  2.5 0.0 copy-start.2
  2.5 0.9 %copy-done.2 = f32[2,16,16,128]{3,2,1,0:T(8,128)S(1)} copy-done((f32[2,16,16,128]{3,2,1,0:T(8,128)S(1)}, f32[2,16,16,128]{3,2,1,0:T(8,128)}, u32[]{:S(2)}) %copy-start.2) | copy-done | bytes 262168
  3.5 0.0 copy-start.3
  3.5 0.9 %copy-done.3 = s32[16,16,128]{2,1,0:T(8,128)S(1)} copy-done((s32[16,16,128]{2,1,0:T(8,128)S(1)}, s32[16,16,128]{2,1,0:T(8,128)}, u32[]{:S(2)}) %copy-start.3) | copy-done | bytes 131096
  4.4 0.0 copy-start.4
  4.4 0.7 %copy-done.4 = f32[8]{0:T(128)S(1)} copy-done((f32[8]{0:T(128)S(1)}, f32[8]{0:T(128)}, u32[]{:S(2)}) %copy-start.4) | copy-done | bytes 56
  5.0 0.0 copy-start.5
  5.0 0.7 %copy-done.5 = f32[8]{0:T(128)S(1)} copy-done((f32[8]{0:T(128)S(1)}, f32[8]{0:T(128)}, u32[]{:S(2)}) %copy-start.5) | copy-done | bytes 56
  5.7 53.6 %shard_map.85 = (f32[2,16,16,128]{3,2,1,0:T(8,128)S(1)}, f32[1,128]{1,0:T(1,128)S(1)}) custom-call(f32[2,16,16,128]{3,2,1,0:T(8,128)S(1)} %copy-done, f32[2,16,16,128]{3,2,1,0:T(8,128)S(1)} %copy-done.1, f32[2,16,16,128]{3,2,1,0:T(8,128)S(1)} %copy-done.2, s32[16,16,128]{2,1,0:T(8,128)S(1)} %copy-done.3, f32[8]{0:T(128)S(1)} %copy-done.4, f32[8]{0:T(128)S(1)} %copy-done.5), custom_call_target="tpu_custom_call" | custom-call | tf_op jit(solution)/shard_map/pallas_call | solution.py:542
  59.3 0.6 slice_bitcast_fusion
  59.9 0.6 %reshape_squeeze.3 = f32[2,8]{1,0:T(2,128)} reshape(f32[16]{0:T(128)S(1)} %slice_reduce_fusion) | data formatting | bytes 128 | tf_op jit(solution)/shard_map/reshape;squeeze | solution.py:586
  60.6 0.7 %copy.10 = f32[2,16,16,128]{3,2,1,0:T(8,128)} copy(f32[2,16,16,128]{3,2,1,0:T(8,128)S(1)} %get-tuple-element.10) | data formatting | bytes 524288
  (1 shorter events, 0.0 us)
Async XLA Ops:
  0.6 1.0 %copy-start = (f32[2,16,16,128]{3,2,1,0:T(8,128)S(1)}, f32[2,16,16,128]{3,2,1,0:T(8,128)}, u32[]{:S(2)}) copy-start(f32[2,16,16,128]{3,2,1,0:T(8,128)} %guess_hbm.1) | copy-start | bytes 786436
  1.6 0.9 %copy-start.1 = (f32[2,16,16,128]{3,2,1,0:T(8,128)S(1)}, f32[2,16,16,128]{3,2,1,0:T(8,128)}, u32[]{:S(2)}) copy-start(f32[2,16,16,128]{3,2,1,0:T(8,128)} %source_hbm.1) | copy-start | bytes 786436
  2.5 0.9 %copy-start.2 = (f32[2,16,16,128]{3,2,1,0:T(8,128)S(1)}, f32[2,16,16,128]{3,2,1,0:T(8,128)}, u32[]{:S(2)}) copy-start(f32[2,16,16,128]{3,2,1,0:T(8,128)} %forward_hbm.1) | copy-start | bytes 786436
  3.5 0.9 %copy-start.3 = (s32[16,16,128]{2,1,0:T(8,128)S(1)}, s32[16,16,128]{2,1,0:T(8,128)}, u32[]{:S(2)}) copy-start(s32[16,16,128]{2,1,0:T(8,128)} %labels_hbm.1) | copy-start | bytes 393220
  4.4 0.7 %copy-start.4 = (f32[8]{0:T(128)S(1)}, f32[8]{0:T(128)}, u32[]{:S(2)}) copy-start(f32[8]{0:T(128)} %pr_ref.1) | copy-start | bytes 100
  5.0 0.7 %copy-start.5 = (f32[8]{0:T(128)S(1)}, f32[8]{0:T(128)}, u32[]{:S(2)}) copy-start(f32[8]{0:T(128)} %pi_ref.1) | copy-start | bytes 100

commit v2 on v1

--- a/solution.py
+++ b/solution.py
@@ -67,6 +67,7 @@
     recv_c,
     send_r,
     recv_r,
+    ready,
 ):
     nx, ny, nz = sizes
     gx, gy, gz = (lax.axis_index(a) for a in AXES)
@@ -90,10 +91,15 @@
 
     y_peers = [(0, dy, 0) for dy in range(1, ny)]
     xz_peers = [(dx, 0, dz) for dx in range(nx) for dz in range(nz) if (dx, dz) != (0, 0)]
-    met = {(dx % nx, dy % ny, dz % nz) for dx, dy, dz in near_offsets() + y_peers + xz_peers}
+
+    def greet(semaphore, offsets):
+        offsets = {(dx % nx, dy % ny, dz % nz) for dx, dy, dz in offsets}
+        for offset in sorted(offsets):
+            pl.semaphore_signal(semaphore, inc=1, device_id=device(offset), device_id_type=MESH)
+        return len(offsets)
+
     barrier = pltpu.get_barrier_semaphore()
-    for offset in sorted(met):
-        pl.semaphore_signal(barrier, inc=1, device_id=device(offset), device_id_type=MESH)
+    met = greet(barrier, near_offsets())
 
     lane = lax.broadcasted_iota(jnp.int32, (8, 128), 1)
     row8 = lax.broadcasted_iota(jnp.int32, (8, 128), 0)
@@ -148,7 +154,7 @@
             ER[z, 8 * yh : 8 * yh + 8] = er
         return carry
 
-    lax.fori_loop(0, 16, own_coefficients, 0)
+    lax.fori_loop(0, 16, own_coefficients, 0, unroll=4)
 
     def own_coarse(zc, carry):
         for yh in range(2):
@@ -159,7 +165,7 @@
             G[1, 0, zc + 2, 8 + 8 * yh : 16 + 8 * yh] = -q4 * scale
         return carry
 
-    lax.fori_loop(0, 8, own_coarse, 0)
+    lax.fori_loop(0, 8, own_coarse, 0, unroll=4)
 
     def pack(pieces):
         total = jnp.zeros((8, 128), F32)
@@ -180,7 +186,7 @@
             PU[zq, yh] = pack([F[f, 0, 4 + 4 * zq + p, rows] for f in range(4) for p in range(4)])
         return carry
 
-    lax.fori_loop(0, 4, pack_quarter, 0)
+    lax.fori_loop(0, 4, pack_quarter, 0, unroll=2)
 
     def planes(dz, own, deep, at):
         if dz == 0:
@@ -204,7 +210,7 @@
         copy.start()
         started.append(copy)
 
-    pl.semaphore_wait(barrier, len(met))
+    pl.semaphore_wait(barrier, met)
 
     for offset in near_offsets():
         dx, dy, dz = offset
@@ -227,9 +233,13 @@
     for offset in ((1, 0, 0), (-1, 0, 0)):
         send(offset, PG, RG.at[0 if offset[0] > 0 else 1], send_a, recv_a)
 
+    met = greet(ready.at[0], [o for o in near_offsets() if o[1] == 0 or (o[0], o[2]) == (0, 0)])
+
     for copy in started:
         copy.wait()
     loads[3].wait()
+    pl.semaphore_wait(ready.at[0], met)
+    met = greet(ready.at[1], [(2, 0, 0), (-2, 0, 0), (0, 2, 0), (0, -2, 0)])
 
     def merged(low, high):
         return jnp.where(left_half, low, high) * slot_ok
@@ -243,7 +253,7 @@
                     F[f, 1, 4 * zq + p, 8 * yg : 8 * yg + 8] = pltpu.roll(both, (124 - 8 * slot) % 128, 1)
         return carry
 
-    lax.fori_loop(0, 6, unpack_quarter, 0)
+    lax.fori_loop(0, 6, unpack_quarter, 0, unroll=6)
 
     y_ok = [(gy > 0).astype(F32), 1.0, 1.0, (gy < ny - 1).astype(F32)]
 
@@ -266,7 +276,7 @@
             H[1, 0, z, rows] = hi * ok
         return carry
 
-    lax.fori_loop(1, 23, halo_coefficients, 0)
+    lax.fori_loop(1, 23, halo_coefficients, 0, unroll=11)
 
     def halo_planes(z, carry):
         low_ok, high_ok = (gz > 0).astype(F32), (gz < nz - 1).astype(F32)
@@ -278,7 +288,7 @@
                 H[1, 0, at, rows] = hi * ok
         return carry
 
-    lax.fori_loop(1, 4, halo_planes, 0)
+    lax.fori_loop(1, 4, halo_planes, 0, unroll=3)
 
     @pl.when(gz == 0)
     def _():
@@ -340,11 +350,14 @@
                     target[1, t, z, mid] = 0.5 * centre[1][t] + (hr * wi + hi * wr)
             return carry
 
-        lax.fori_loop(first, last, plane, 0)
+        lax.fori_loop(first, last, plane, 0, unroll=(last - first) // 2)
 
     sweep(F, B, 1, 23)
     sweep(B, F, 2, 22)
     sweep(F, B, 3, 21)
+
+    pl.semaphore_wait(ready.at[1], met)
+    met = greet(ready.at[2], [(0, 4, 0), (0, -4, 0)])
 
     zero = jnp.zeros((8, 128), F32)
 
@@ -381,7 +394,7 @@
             E[1, 0, zc + 2, mid] = wr * bi + wi * br
         return src_sq, pre_sq
 
-    src_sq, pre_sq = lax.fori_loop(0, 8, residual, (zero, zero))
+    src_sq, pre_sq = lax.fori_loop(0, 8, residual, (zero, zero), unroll=4)
 
     for yh in range(2):
         PE[yh] = pack([E[c, 0, 2 + z, 8 + 8 * yh : 16 + 8 * yh] for c in range(2) for z in range(8)])
@@ -452,7 +465,7 @@
         coarse(zc, (4, 20), 1)
         return carry
 
-    lax.fori_loop(2, 10, own_planes, 0)
+    lax.fori_loop(2, 10, own_planes, 0, unroll=4)
     coarse(1, (8, 16), 1)
     coarse(10, (8, 16), 1)
 
@@ -489,9 +502,11 @@
                     carry[9 + m] = carry[9 + m] + jnp.where(chosen, pi, 0.0)
         return tuple(carry)
 
-    sums = lax.fori_loop(0, 8, correct, (zero,) * 17)
+    sums = lax.fori_loop(0, 8, correct, (zero,) * 17, unroll=2)
     store = pltpu.make_async_copy(ADJ, adj_hbm, local_sem.at[0])
     store.start()
+
+    pl.semaphore_wait(ready.at[2], met)
 
     ordered = list(sums[1:]) + [src_sq, pre_sq, sums[0]]
     ACC[...] = jnp.zeros((24, 128), F32)
@@ -535,6 +550,14 @@
     store.wait()
 
 
+def finish(adjoint, row_ref, out, grad, norms):
+    out[...] = adjoint[...]
+    row = row_ref[...]
+    grad[0:1] = row[:, :NMAT]
+    grad[1:2] = pltpu.roll(row, 128 - NMAT, 1)[:, :NMAT]
+    norms[...] = pltpu.roll(row, 128 - 2 * NMAT, 1)[0, :3]
+
+
 def shards(sizes, source, adjoint_guess, forward_field, labels, perm_real, perm_imag):
     vmem = lambda *shape: pltpu.VMEM(shape, F32)
     dma = pltpu.SemaphoreType.DMA
@@ -545,8 +568,8 @@
             jax.ShapeDtypeStruct(adjoint_guess.shape, F32),
             jax.ShapeDtypeStruct((1, 128), F32),
         ),
-        in_specs=[pl.BlockSpec(memory_space=pl.ANY)] * 4 + [pl.BlockSpec(memory_space=pltpu.SMEM)] * 2,
-        out_specs=(pl.BlockSpec(memory_space=pl.ANY), pl.BlockSpec(memory_space=pltpu.VMEM)),
+        in_specs=[pl.BlockSpec(memory_space=pltpu.HBM)] * 4 + [pl.BlockSpec(memory_space=pltpu.SMEM)] * 2,
+        out_specs=(pl.BlockSpec(memory_space=pltpu.HBM), pl.BlockSpec(memory_space=pltpu.VMEM)),
         scratch_shapes=[
             vmem(5, 2, 24, 32, 128),
             vmem(2, 2, 24, 32, 128),
@@ -580,12 +603,20 @@
             dma((n_c,)),
             dma((2,)),
             dma((2,)),
+            pltpu.SemaphoreType.REGULAR((3,)),
         ],
-        compiler_params=pltpu.CompilerParams(collective_id=0, has_side_effects=True, vmem_limit_bytes=40 << 20),
+        compiler_params=pltpu.CompilerParams(collective_id=0, has_side_effects=True, vmem_limit_bytes=60 << 20),
     )(adjoint_guess, source, forward_field, labels, perm_real, perm_imag)
-    material_grad = row[0, : 2 * NMAT].reshape(2, NMAT)
-    norms = row[0, 2 * NMAT : 2 * NMAT + 3]
-    return adjoint, material_grad, norms
+    return pl.pallas_call(
+        finish,
+        out_shape=(
+            jax.ShapeDtypeStruct(adjoint_guess.shape, F32),
+            jax.ShapeDtypeStruct((2, NMAT), F32),
+            jax.ShapeDtypeStruct((3,), F32),
+        ),
+        in_specs=[pl.BlockSpec(memory_space=pltpu.VMEM)] * 2,
+        out_specs=(pl.BlockSpec(memory_space=pltpu.VMEM),) * 3,
+    )(adjoint, row)
 
 
 def solution(mesh):

time: 61.5 us -> 47.9 us (0.78)
  local copies, waits for them, and re-layouts: 7 us -> 0 us
  Pallas kernels: 53.6 us -> 47.1 us
    pallas_call x1, Pallas kernels: 53.6 us -> 45.4 us  [shards(): pl.pallas_call(functools.partial(kernel, sizes), out_shape=(jax.ShapeDtyp...]
    unnamed x13 -> x0, local copies, waits for them, and re-layouts: 5.76 us -> none
    pallas_call x0 -> x1, Pallas kernels: none -> 1.68 us  [shards(): pl.pallas_call(finish, out_shape=(jax.ShapeDtypeStruct(adjoint_guess.shap...]
    another operation x1 -> x0, local copies, waits for them, and re-layouts: 0.64 us -> none  [shards(): material_grad = row[0, :2 * NMAT].reshape(2, NMAT)]
where the time goes in v2:
time: 47.9 us; the launch traced here: 47.7 us
  Pallas kernels  47.1 us (98%)
  between operations  0.64 us (1%)
    pallas_call x1, Pallas kernels, shards(): pl.pallas_call(functools.partial(kernel, sizes), out_shape=(jax.ShapeDtyp...  45.4 us
    pallas_call x1, Pallas kernels, shards(): pl.pallas_call(finish, out_shape=(jax.ShapeDtypeStruct(adjoint_guess.shap...  1.68 us

profile of v2, /device:TPU:1, one launch (start us, length us, event | category | flops | bytes accessed | tf_op | source)
XLA Modules:
  0.0 47.7 jit_solution(13219899374229608771)
XLA Ops:
  0.6 45.4 %shard_map.85 = (f32[2,16,16,128]{3,2,1,0:T(8,128)}, f32[1,128]{1,0:T(1,128)}) custom-call(f32[2,16,16,128]{3,2,1,0:T(8,128)} %guess_hbm.1, f32[2,16,16,128]{3,2,1,0:T(8,128)} %source_hbm.1, f32[2,16,16,128]{3,2,1,0:T(8,128)} %forward_hbm.1, s32[16,16,128]{2,1,0:T(8,128)} %labels_hbm.1, f32[8]{0:T(128)} %pr_ref.1, f32[8]{0:T(128)} %pi_ref.1), custom_call_target="tpu_custom_call" | custom-call | tf_op jit(solution)/shard_map/pallas_call | solution.py:565
  46.1 1.7 %shard_map.86 = (f32[2,16,16,128]{3,2,1,0:T(8,128)}, f32[2,8]{1,0:T(2,128)}, f32[3]{0:T(128)}) custom-call(f32[2,16,16,128]{3,2,1,0:T(8,128)} %get-tuple-element.5.adjoint, f32[1,128]{1,0:T(1,128)} %get-tuple-element.6.row_ref), custom_call_target="tpu_custom_call" | custom-call | tf_op jit(solution)/shard_map/pallas_call | solution.py:610

commit v3 on v2

--- a/solution.py
+++ b/solution.py
@@ -52,8 +52,10 @@
     PL,
     PG,
     PE,
+    PZ,
     RU,
     RL,
+    RZ,
     RG,
     RE,
     ACC,
@@ -92,6 +94,9 @@
     y_peers = [(0, dy, 0) for dy in range(1, ny)]
     xz_peers = [(dx, 0, dz) for dx in range(nx) for dz in range(nz) if (dx, dz) != (0, 0)]
 
+    y_peers.sort(key=lambda o: -min(o[1], ny - o[1]))
+    xz_peers.sort(key=lambda o: -(min(o[0], nx - o[0]) + min(o[2], nz - o[2])))
+
     def greet(semaphore, offsets):
         offsets = {(dx % nx, dy % ny, dz % nz) for dx, dy, dz in offsets}
         for offset in sorted(offsets):
@@ -111,6 +116,9 @@
     right_ok = (gx < nx - 1).astype(F32)
     side_ok = jnp.where(lane < 64, right_ok, left_ok)
     slot_ok = jnp.where(left_half, left_ok, right_ok)
+    low_y_ok, high_y_ok = (gy > 0).astype(F32), (gy < ny - 1).astype(F32)
+    low_z_ok, high_z_ok = (gz > 0).astype(F32), (gz < nz - 1).astype(F32)
+    halo_rows_ok = jnp.where(row8 < 4, high_y_ok, low_y_ok)
 
     for m in range(NMAT):
         er = jnp.full((8, 128), pr_ref[m], F32)
@@ -187,6 +195,13 @@
         return carry
 
     lax.fori_loop(0, 4, pack_quarter, 0, unroll=2)
+    edge_slots = [(0, 3), (1, 3), (2, 2), (3, 2), (4, 2)]
+    for up in range(2):
+        for yh in range(2):
+            rows = slice(8 + 8 * yh, 16 + 8 * yh)
+            PZ[up, yh] = pack(
+                [F[f, 0, (20 - deep + p) if up else 4 + p, rows] for f, deep in edge_slots for p in range(deep)]
+            )
 
     def planes(dz, own, deep, at):
         if dz == 0:
@@ -212,20 +227,33 @@
 
     pl.semaphore_wait(barrier, met)
 
-    for offset in near_offsets():
+    def tiles(dy):
+        if dy == 0:
+            return pl.ds(0, 2), pl.ds(0, 2), pl.ds(0, 8)
+        if dy > 0:
+            return pl.ds(1, 1), pl.ds(2, 1), pl.ds(4, 4)
+        return pl.ds(0, 1), pl.ds(2, 1), pl.ds(0, 4)
+
+    def send_fine(offset):
         dx, dy, dz = offset
         if dx == 0:
-            from_z, to_z = planes(dz, 16, 4, 4)
-            from_y, to_y = planes(dy, 16, 4, 8)
-            send(offset, F.at[:, 0, from_z, from_y], F.at[:, 0, to_z, to_y], send_a, recv_a)
+            for fields, deep in ((pl.ds(0, 2), 4), (pl.ds(2, 3), 3)):
+                deep = deep - 1 if dy and dz else deep
+                from_z, to_z = planes(dz, 16, deep, 4)
+                from_y, to_y = planes(dy, 16, deep, 8)
+                send(offset, F.at[fields, 0, from_z, from_y], F.at[fields, 0, to_z, to_y], send_a, recv_a)
+            return
+        side = 0 if dx > 0 else 1
+        from_y, to_y, rows = tiles(dy)
+        if dz:
+            up = 1 if dz > 0 else 0
+            send(offset, PZ.at[up, from_y, rows], RZ.at[side, 1 - up, to_y, rows], send_a, recv_a)
         else:
-            side = 0 if dx > 0 else 1
-            from_z, to_z = planes(dz, 4, 1, 1)
-            from_y, to_y = planes(dy, 2, 1, 1)
-            from_z = pl.ds(from_z.start - 1, from_z.size)
-            from_y = pl.ds(from_y.start - 1, from_y.size)
-            send(offset, PU.at[from_z, from_y], RU.at[side, to_z, to_y], send_a, recv_a)
-            send(offset, PL.at[from_y], RL.at[side, 1 - dz, to_y], send_a, recv_a)
+            send(offset, PU.at[:, from_y, rows], RU.at[side, :, to_y, rows], send_a, recv_a)
+            send(offset, PL.at[from_y, rows], RL.at[side, to_y, rows], send_a, recv_a)
+
+    for offset in sorted(near_offsets(), key=lambda o: (o[:2] != (0, 0), -sum(abs(d) for d in o))):
+        send_fine(offset)
     for offset in ((0, 0, 1), (0, 0, -1), (0, 1, 0), (0, -1, 0)):
         from_z, to_z = planes(offset[2], 8, 1, 2)
         from_y, to_y = planes(offset[1], 16, 4, 8)
@@ -244,51 +272,66 @@
     def merged(low, high):
         return jnp.where(left_half, low, high) * slot_ok
 
+    def spread(ref, index, tile, value):
+        if tile < 2:
+            ref[(*index, slice(8 + 8 * tile, 16 + 8 * tile))] = value
+        else:
+            ref[(*index, slice(24, 28))] = value[0:4]
+            ref[(*index, slice(4, 8))] = value[4:8]
+
+    def from_slot(packed, slot):
+        return pltpu.roll(packed, (124 - 8 * slot) % 128, 1)
+
+    for up in range(2):
+        for tile in range(3):
+            both = merged(RZ[0, up, tile], RZ[1, up, tile])
+            ok = side_ok * (high_z_ok if up else low_z_ok)
+            ok = ok * halo_rows_ok if tile == 2 else ok
+            slot = 0
+            for f, deep in edge_slots:
+                for p in range(deep):
+                    at = 20 + p if up else 4 - deep + p
+                    piece = from_slot(both, slot)
+                    slot += 1
+                    if f < 4:
+                        spread(F, (f, 1, at), tile, piece)
+                    else:
+                        hr, hi = look_up(piece, (0, 1))
+                        spread(H, (0, 1, at), tile, hr * ok)
+                        spread(H, (1, 1, at), tile, hi * ok)
+        for p in range(3):
+            at = 20 + p if up else 1 + p
+            ok = high_z_ok if up else low_z_ok
+            for yg, y_ok in enumerate((low_y_ok, 1.0, 1.0, high_y_ok)):
+                rows = slice(8 * yg, 8 * yg + 8)
+                hr, hi = look_up(F[4, 0, at, rows], (0, 1))
+                H[0, 0, at, rows] = hr * (ok * y_ok)
+                H[1, 0, at, rows] = hi * (ok * y_ok)
+
     def unpack_quarter(zq, carry):
-        for yg in range(4):
-            both = merged(RU[0, zq, yg], RU[1, zq, yg])
+        for tile in range(3):
+            both = merged(RU[0, zq, tile], RU[1, zq, tile])
             for f in range(4):
                 for p in range(4):
-                    slot = 4 * f + p
-                    F[f, 1, 4 * zq + p, 8 * yg : 8 * yg + 8] = pltpu.roll(both, (124 - 8 * slot) % 128, 1)
+                    spread(F, (f, 1, 4 + 4 * zq + p), tile, from_slot(both, 4 * f + p))
         return carry
 
-    lax.fori_loop(0, 6, unpack_quarter, 0, unroll=6)
-
-    y_ok = [(gy > 0).astype(F32), 1.0, 1.0, (gy < ny - 1).astype(F32)]
+    lax.fori_loop(0, 4, unpack_quarter, 0, unroll=4)
 
     def halo_coefficients(z, carry):
-        z_ok = ((z >= 4) | (gz > 0)).astype(F32) * ((z < 20) | (gz < nz - 1)).astype(F32)
-        part = (z + 12) // 16
-        shift = 124 - 8 * lax.rem(z + 12, 16)
-        for yg in range(4):
-            rows = slice(8 * yg, 8 * yg + 8)
-            label = pltpu.roll(merged(RL[0, part, yg], RL[1, part, yg]), shift, 1)
-            hr, hi = look_up(label, (0, 1))
-            ok = side_ok * (z_ok * y_ok[yg])
-            H[0, 1, z, rows] = hr * ok
-            H[1, 1, z, rows] = hi * ok
-        for yg in (0, 3):
-            rows = slice(8 * yg, 8 * yg + 8)
+        shift = 124 - 8 * (z - 4)
+        for tile in range(3):
+            hr, hi = look_up(pltpu.roll(merged(RL[0, tile], RL[1, tile]), shift, 1), (0, 1))
+            ok = side_ok * halo_rows_ok if tile == 2 else side_ok
+            spread(H, (0, 1, z), tile, hr * ok)
+            spread(H, (1, 1, z), tile, hi * ok)
+        for rows, ok in ((slice(0, 8), low_y_ok), (slice(24, 32), high_y_ok)):
             hr, hi = look_up(F[4, 0, z, rows], (0, 1))
-            ok = z_ok * y_ok[yg]
             H[0, 0, z, rows] = hr * ok
             H[1, 0, z, rows] = hi * ok
         return carry
 
-    lax.fori_loop(1, 23, halo_coefficients, 0, unroll=11)
-
-    def halo_planes(z, carry):
-        low_ok, high_ok = (gz > 0).astype(F32), (gz < nz - 1).astype(F32)
-        for at, ok in ((z, low_ok), (z + 19, high_ok)):
-            for yg in (1, 2):
-                rows = slice(8 * yg, 8 * yg + 8)
-                hr, hi = look_up(F[4, 0, at, rows], (0, 1))
-                H[0, 0, at, rows] = hr * ok
-                H[1, 0, at, rows] = hi * ok
-        return carry
-
-    lax.fori_loop(1, 4, halo_planes, 0, unroll=3)
+    lax.fori_loop(4, 20, halo_coefficients, 0, unroll=8)
 
     @pl.when(gz == 0)
     def _():
@@ -302,13 +345,13 @@
 
     @pl.when(gy == 0)
     def _():
-        F[0:2, :, :, 0:8] = jnp.zeros((2, 2, 24, 8, 128), F32)
-        G[:, 0, :, 0:8] = jnp.zeros((2, 12, 8, 128), F32)
+        F[0:2, :, :, 4:8] = jnp.zeros((2, 2, 24, 4, 128), F32)
+        G[:, 0, :, 4:8] = jnp.zeros((2, 12, 4, 128), F32)
 
     @pl.when(gy == ny - 1)
     def _():
-        F[0:2, :, :, 24:32] = jnp.zeros((2, 2, 24, 8, 128), F32)
-        G[:, 0, :, 24:32] = jnp.zeros((2, 12, 8, 128), F32)
+        F[0:2, :, :, 24:28] = jnp.zeros((2, 2, 24, 4, 128), F32)
+        G[:, 0, :, 24:28] = jnp.zeros((2, 12, 4, 128), F32)
 
     for yh in range(2):
         both = merged(RG[0, yh], RG[1, yh])
@@ -409,19 +452,18 @@
             send(offset, E.at[:, 0, from_z, from_y], E.at[:, 0, to_z, to_y], send_c, recv_c)
         else:
             side = 0 if dx > 0 else 1
-            from_y, to_y = planes(dy, 2, 1, 1)
-            from_y = pl.ds(from_y.start - 1, from_y.size)
-            send(offset, PE.at[from_y], RE.at[side, 1 - dz, to_y], send_c, recv_c)
+            from_y, to_y, rows = tiles(dy)
+            send(offset, PE.at[from_y, rows], RE.at[side, 1 - dz, to_y, rows], send_c, recv_c)
     for copy in started:
         copy.wait()
 
     for part, where in ((1, range(8)), (0, (7,)), (2, (0,))):
-        for yg in range(4) if part == 1 else (1, 2):
-            both = merged(RE[0, part, yg], RE[1, part, yg])
+        for tile in range(3 if part == 1 else 2):
+            both = merged(RE[0, part, tile], RE[1, part, tile])
             for c in range(2):
                 for z in where:
                     at = 2 + z if part == 1 else (1 if part == 0 else 10)
-                    E[c, 1, at, 8 * yg : 8 * yg + 8] = pltpu.roll(both, (124 - 8 * (8 * c + z)) % 128, 1)
+                    spread(E, (c, 1, at), tile, from_slot(both, 8 * c + z))
 
     @pl.when(gz == 0)
     def _():
@@ -433,11 +475,11 @@
 
     @pl.when(gy == 0)
     def _():
-        E[:, :, :, 0:8] = jnp.zeros((2, 2, 12, 8, 128), F32)
+        E[:, :, :, 4:8] = jnp.zeros((2, 2, 12, 4, 128), F32)
 
     @pl.when(gy == ny - 1)
     def _():
-        E[:, :, :, 24:32] = jnp.zeros((2, 2, 12, 8, 128), F32)
+        E[:, :, :, 24:28] = jnp.zeros((2, 2, 12, 4, 128), F32)
 
     def coarse(zc, row_groups, tiles):
         for rows in row_groups:
@@ -588,10 +630,12 @@
             vmem(2, 8, 128),
             vmem(2, 8, 128),
             vmem(2, 8, 128),
-            vmem(2, 6, 4, 8, 128),
-            vmem(2, 3, 4, 8, 128),
             vmem(2, 2, 8, 128),
-            vmem(2, 3, 4, 8, 128),
+            vmem(2, 4, 3, 8, 128),
+            vmem(2, 3, 8, 128),
+            vmem(2, 2, 3, 8, 128),
+            vmem(2, 2, 8, 128),
+            vmem(2, 3, 3, 8, 128),
             vmem(24, 128),
             vmem(2, 1, 128),
             vmem(sizes[1], 1, 128),

time: 47.9 us -> 45.2 us (0.944)
  Pallas kernels: 47.1 us -> 44.4 us
    pallas_call x1, Pallas kernels: 45.4 us -> 42.7 us  [shards(): pl.pallas_call(functools.partial(kernel, sizes), out_shape=(jax.ShapeDtyp...]
where the time goes in v3:
time: 45.2 us; the launch traced here: 45.1 us
  Pallas kernels  44.4 us (98%)
  between operations  0.64 us (1%)
    pallas_call x1, Pallas kernels, shards(): pl.pallas_call(functools.partial(kernel, sizes), out_shape=(jax.ShapeDtyp...  42.7 us
    pallas_call x1, Pallas kernels, shards(): pl.pallas_call(finish, out_shape=(jax.ShapeDtypeStruct(adjoint_guess.shap...  1.68 us

profile of v3, /device:TPU:1, one launch (start us, length us, event | category | flops | bytes accessed | tf_op | source)
XLA Modules:
  0.0 45.1 jit_solution(4660774532568735166)
XLA Ops:
  0.6 42.7 %shard_map.85 = (f32[2,16,16,128]{3,2,1,0:T(8,128)}, f32[1,128]{1,0:T(1,128)}) custom-call(f32[2,16,16,128]{3,2,1,0:T(8,128)} %guess_hbm.1, f32[2,16,16,128]{3,2,1,0:T(8,128)} %source_hbm.1, f32[2,16,16,128]{3,2,1,0:T(8,128)} %forward_hbm.1, s32[16,16,128]{2,1,0:T(8,128)} %labels_hbm.1, f32[8]{0:T(128)} %pr_ref.1, f32[8]{0:T(128)} %pi_ref.1), custom_call_target="tpu_custom_call" | custom-call | tf_op jit(solution)/shard_map/pallas_call | solution.py:607
  43.4 1.7 %shard_map.86 = (f32[2,16,16,128]{3,2,1,0:T(8,128)}, f32[2,8]{1,0:T(2,128)}, f32[3]{0:T(128)}) custom-call(f32[2,16,16,128]{3,2,1,0:T(8,128)} %get-tuple-element.5.adjoint, f32[1,128]{1,0:T(1,128)} %get-tuple-element.6.row_ref), custom_call_target="tpu_custom_call" | custom-call | tf_op jit(solution)/shard_map/pallas_call | solution.py:654

commit v4 on v3

--- a/solution.py
+++ b/solution.py
@@ -120,18 +120,6 @@
     low_z_ok, high_z_ok = (gz > 0).astype(F32), (gz < nz - 1).astype(F32)
     halo_rows_ok = jnp.where(row8 < 4, high_y_ok, low_y_ok)
 
-    for m in range(NMAT):
-        er = jnp.full((8, 128), pr_ref[m], F32)
-        ei = jnp.full((8, 128), pi_ref[m], F32)
-        dr = 6.0 - KH2 * (er + SHIFT * ei)
-        di = -KH2 * (SHIFT * er - ei)
-        half = 0.5 / (dr * dr + di * di)
-        TB[0, m] = dr * half
-        TB[1, m] = -di * half
-        TB[2, m] = dr
-        TB[3, m] = di
-        TB[4, m] = er
-
     def look_up(label, tables):
         high = label >= 3.5
         rest = jnp.where(high, label - 4.0, label)
@@ -149,31 +137,7 @@
         return v + jnp.where(even_lane, pltpu.roll(v, 127, 1), pltpu.roll(v, 1, 1))
 
     loads[0].wait()
-
-    def own_coefficients(z, carry):
-        for yh in range(2):
-            label = LI[z, 8 * yh : 8 * yh + 8].astype(F32)
-            F[4, 0, z + 4, 8 + 8 * yh : 16 + 8 * yh] = label
-            hr, hi, dr, di, er = look_up(label, (0, 1, 2, 3, 4))
-            H[0, 0, z + 4, 8 + 8 * yh : 16 + 8 * yh] = hr
-            H[1, 0, z + 4, 8 + 8 * yh : 16 + 8 * yh] = hi
-            D[0, z, 8 * yh : 8 * yh + 8] = dr
-            D[1, z, 8 * yh : 8 * yh + 8] = di
-            ER[z, 8 * yh : 8 * yh + 8] = er
-        return carry
-
-    lax.fori_loop(0, 16, own_coefficients, 0, unroll=4)
-
-    def own_coarse(zc, carry):
-        for yh in range(2):
-            rows = slice(8 * yh, 8 * yh + 8)
-            q4 = (KH2 * 4.0 / 8.0) * block_sum(ER[2 * zc, rows] + ER[2 * zc + 1, rows])
-            scale = 0.5 / (36.0 + q4 * q4)
-            G[0, 0, zc + 2, 8 + 8 * yh : 16 + 8 * yh] = 6.0 * scale
-            G[1, 0, zc + 2, 8 + 8 * yh : 16 + 8 * yh] = -q4 * scale
-        return carry
-
-    lax.fori_loop(0, 8, own_coarse, 0, unroll=4)
+    F[4, 0, 4:20, 8:24] = LI[...].astype(F32)
 
     def pack(pieces):
         total = jnp.zeros((8, 128), F32)
@@ -184,7 +148,6 @@
     for yh in range(2):
         rows = slice(8 + 8 * yh, 16 + 8 * yh)
         PL[yh] = pack([F[4, 0, 4 + z, rows] for z in range(16)])
-        PG[yh] = pack([G[c, 0, 2 + z, rows] for c in range(2) for z in range(8)])
     loads[1].wait()
     loads[2].wait()
 
@@ -234,10 +197,10 @@
             return pl.ds(1, 1), pl.ds(2, 1), pl.ds(4, 4)
         return pl.ds(0, 1), pl.ds(2, 1), pl.ds(0, 4)
 
-    def send_fine(offset):
+    def send_fine(offset, parts):
         dx, dy, dz = offset
         if dx == 0:
-            for fields, deep in ((pl.ds(0, 2), 4), (pl.ds(2, 3), 3)):
+            for fields, deep in parts:
                 deep = deep - 1 if dy and dz else deep
                 from_z, to_z = planes(dz, 16, deep, 4)
                 from_y, to_y = planes(dy, 16, deep, 8)
@@ -245,15 +208,61 @@
             return
         side = 0 if dx > 0 else 1
         from_y, to_y, rows = tiles(dy)
-        if dz:
+        if len(parts) == 2:
+            if dz == 0:
+                send(offset, PU.at[:, from_y, rows], RU.at[side, :, to_y, rows], send_a, recv_a)
+        elif dz == 0:
+            send(offset, PL.at[from_y, rows], RL.at[side, to_y, rows], send_a, recv_a)
+        else:
             up = 1 if dz > 0 else 0
             send(offset, PZ.at[up, from_y, rows], RZ.at[side, 1 - up, to_y, rows], send_a, recv_a)
-        else:
-            send(offset, PU.at[:, from_y, rows], RU.at[side, :, to_y, rows], send_a, recv_a)
-            send(offset, PL.at[from_y, rows], RL.at[side, to_y, rows], send_a, recv_a)
-
-    for offset in sorted(near_offsets(), key=lambda o: (o[:2] != (0, 0), -sum(abs(d) for d in o))):
-        send_fine(offset)
+
+    order = sorted(near_offsets(), key=lambda o: (o[:2] != (0, 0), -sum(abs(d) for d in o)))
+    for offset in order:
+        send_fine(offset, [(pl.ds(4, 1), 3)])
+    first_group = list(started)
+    for offset in order:
+        send_fine(offset, [(pl.ds(0, 2), 4), (pl.ds(2, 2), 3)])
+
+    for m in range(NMAT):
+        er = jnp.full((8, 128), pr_ref[m], F32)
+        ei = jnp.full((8, 128), pi_ref[m], F32)
+        dr = 6.0 - KH2 * (er + SHIFT * ei)
+        di = -KH2 * (SHIFT * er - ei)
+        half = 0.5 / (dr * dr + di * di)
+        TB[0, m] = dr * half
+        TB[1, m] = -di * half
+        TB[2, m] = dr
+        TB[3, m] = di
+        TB[4, m] = er
+
+    def own_coefficients(z, carry):
+        for yh in range(2):
+            label = F[4, 0, z + 4, 8 + 8 * yh : 16 + 8 * yh]
+            hr, hi, dr, di, er = look_up(label, (0, 1, 2, 3, 4))
+            H[0, 0, z + 4, 8 + 8 * yh : 16 + 8 * yh] = hr
+            H[1, 0, z + 4, 8 + 8 * yh : 16 + 8 * yh] = hi
+            D[0, z, 8 * yh : 8 * yh + 8] = dr
+            D[1, z, 8 * yh : 8 * yh + 8] = di
+            ER[z, 8 * yh : 8 * yh + 8] = er
+        return carry
+
+    lax.fori_loop(0, 16, own_coefficients, 0, unroll=4)
+
+    def own_coarse(zc, carry):
+        for yh in range(2):
+            rows = slice(8 * yh, 8 * yh + 8)
+            q4 = (KH2 * 4.0 / 8.0) * block_sum(ER[2 * zc, rows] + ER[2 * zc + 1, rows])
+            scale = 0.5 / (36.0 + q4 * q4)
+            G[0, 0, zc + 2, 8 + 8 * yh : 16 + 8 * yh] = 6.0 * scale
+            G[1, 0, zc + 2, 8 + 8 * yh : 16 + 8 * yh] = -q4 * scale
+        return carry
+
+    lax.fori_loop(0, 8, own_coarse, 0, unroll=4)
+
+    for yh in range(2):
+        rows = slice(8 + 8 * yh, 16 + 8 * yh)
+        PG[yh] = pack([G[c, 0, 2 + z, rows] for c in range(2) for z in range(8)])
     for offset in ((0, 0, 1), (0, 0, -1), (0, 1, 0), (0, -1, 0)):
         from_z, to_z = planes(offset[2], 8, 1, 2)
         from_y, to_y = planes(offset[1], 16, 4, 8)
@@ -263,11 +272,8 @@
 
     met = greet(ready.at[0], [o for o in near_offsets() if o[1] == 0 or (o[0], o[2]) == (0, 0)])
 
-    for copy in started:
+    for copy in first_group:
         copy.wait()
-    loads[3].wait()
-    pl.semaphore_wait(ready.at[0], met)
-    met = greet(ready.at[1], [(2, 0, 0), (-2, 0, 0), (0, 2, 0), (0, -2, 0)])
 
     def merged(low, high):
         return jnp.where(left_half, low, high) * slot_ok
@@ -308,16 +314,6 @@
                 H[0, 0, at, rows] = hr * (ok * y_ok)
                 H[1, 0, at, rows] = hi * (ok * y_ok)
 
-    def unpack_quarter(zq, carry):
-        for tile in range(3):
-            both = merged(RU[0, zq, tile], RU[1, zq, tile])
-            for f in range(4):
-                for p in range(4):
-                    spread(F, (f, 1, 4 + 4 * zq + p), tile, from_slot(both, 4 * f + p))
-        return carry
-
-    lax.fori_loop(0, 4, unpack_quarter, 0, unroll=4)
-
     def halo_coefficients(z, carry):
         shift = 124 - 8 * (z - 4)
         for tile in range(3):
@@ -332,6 +328,23 @@
         return carry
 
     lax.fori_loop(4, 20, halo_coefficients, 0, unroll=8)
+
+    for copy in started[len(first_group) :]:
+        copy.wait()
+    loads[3].wait()
+
+    def unpack_quarter(zq, carry):
+        for tile in range(3):
+            both = merged(RU[0, zq, tile], RU[1, zq, tile])
+            for f in range(4):
+                for p in range(4):
+                    spread(F, (f, 1, 4 + 4 * zq + p), tile, from_slot(both, 4 * f + p))
+        return carry
+
+    lax.fori_loop(0, 4, unpack_quarter, 0, unroll=4)
+
+    pl.semaphore_wait(ready.at[0], met)
+    met = greet(ready.at[1], [(2, 0, 0), (-2, 0, 0), (0, 2, 0), (0, -2, 0)])
 
     @pl.when(gz == 0)
     def _():
@@ -603,7 +616,7 @@
 def shards(sizes, source, adjoint_guess, forward_field, labels, perm_real, perm_imag):
     vmem = lambda *shape: pltpu.VMEM(shape, F32)
     dma = pltpu.SemaphoreType.DMA
-    n_a, n_c = 50, 18
+    n_a, n_c = 54, 18
     adjoint, row = pl.pallas_call(
         functools.partial(kernel, sizes),
         out_shape=(
@@ -649,8 +662,8 @@
             dma((2,)),
             pltpu.SemaphoreType.REGULAR((3,)),
         ],
-        compiler_params=pltpu.CompilerParams(collective_id=0, has_side_effects=True, vmem_limit_bytes=60 << 20),
-    )(adjoint_guess, source, forward_field, labels, perm_real, perm_imag)
+        compiler_params=pltpu.CompilerParams(collective_id=0, has_side_effects=True, vmem_limit_bytes=20 << 20),
+    )(*(pltpu.with_memory_space_constraint(a, pltpu.HBM) for a in (adjoint_guess, source, forward_field, labels, perm_real, perm_imag)))
     return pl.pallas_call(
         finish,
         out_shape=(
@@ -660,7 +673,7 @@
         ),
         in_specs=[pl.BlockSpec(memory_space=pltpu.VMEM)] * 2,
         out_specs=(pl.BlockSpec(memory_space=pltpu.VMEM),) * 3,
-    )(adjoint, row)
+    )(*(pltpu.with_memory_space_constraint(a, pltpu.VMEM) for a in (adjoint, row)))
 
 
 def solution(mesh):

time: 45.2 us -> 43.4 us (0.960)
  Pallas kernels: 44.4 us -> 42.6 us
    pallas_call x1, Pallas kernels: 1.68 us -> 0.72 us  [shards(): pl.pallas_call(finish, out_shape=(jax.ShapeDtypeStruct(adjoint_guess.shap...]
    pallas_call x1, Pallas kernels: 42.7 us -> 41.8 us  [shards(): pl.pallas_call(functools.partial(kernel, sizes), out_shape=(jax.ShapeDtyp...]
where the time goes in v4:
time: 43.4 us; the launch traced here: 43.2 us
  Pallas kernels  42.6 us (98%)
  between operations  0.64 us (1%)
    pallas_call x1, Pallas kernels, shards(): pl.pallas_call(functools.partial(kernel, sizes), out_shape=(jax.ShapeDtyp...  41.8 us

profile of v4, /device:TPU:1, one launch (start us, length us, event | category | flops | bytes accessed | tf_op | source)
XLA Modules:
  0.0 43.2 jit_solution(15430993122011621777)
XLA Ops:
  0.6 41.8 %shard_map.85 = (f32[2,16,16,128]{3,2,1,0:T(8,128)S(1)}, f32[1,128]{1,0:T(1,128)S(1)}) custom-call(f32[2,16,16,128]{3,2,1,0:T(8,128)} %guess_hbm.1, f32[2,16,16,128]{3,2,1,0:T(8,128)} %source_hbm.1, f32[2,16,16,128]{3,2,1,0:T(8,128)} %forward_hbm.1, s32[16,16,128]{2,1,0:T(8,128)} %labels_hbm.1, f32[8]{0:T(128)} %pr_ref.1, f32[8]{0:T(128)} %pi_ref.1), custom_call_target="tpu_custom_call" | custom-call | tf_op jit(solution)/shard_map/pallas_call | solution.py:620
  42.5 0.7 %shard_map.86 = (f32[2,16,16,128]{3,2,1,0:T(8,128)}, f32[2,8]{1,0:T(2,128)}, f32[3]{0:T(128)}) custom-call(f32[2,16,16,128]{3,2,1,0:T(8,128)S(1)} %get-tuple-element.5.adjoint, f32[1,128]{1,0:T(1,128)S(1)} %get-tuple-element.6.row_ref), custom_call_target="tpu_custom_call" | custom-call | tf_op jit(solution)/shard_map/pallas_call | solution.py:667

commit v5 on v4

--- a/solution.py
+++ b/solution.py
@@ -450,20 +450,20 @@
             E[1, 0, zc + 2, mid] = wr * bi + wi * br
         return src_sq, pre_sq
 
-    src_sq, pre_sq = lax.fori_loop(0, 8, residual, (zero, zero), unroll=4)
-
-    for yh in range(2):
-        PE[yh] = pack([E[c, 0, 2 + z, 8 + 8 * yh : 16 + 8 * yh] for c in range(2) for z in range(8)])
+    src_sq, pre_sq = lax.fori_loop(0, 8, residual, (zero, zero), unroll=8)
+
     del started[:]
-    for offset in near_offsets():
+    for offset in order:
         dx, dy, dz = offset
-        if dx and dy and dz:
-            continue
         if dx == 0:
             from_z, to_z = planes(dz, 8, 1 if dy else 2, 2)
             from_y, to_y = planes(dy, 16, 4, 8)
             send(offset, E.at[:, 0, from_z, from_y], E.at[:, 0, to_z, to_y], send_c, recv_c)
-        else:
+    for yh in range(2):
+        PE[yh] = pack([E[c, 0, 2 + z, 8 + 8 * yh : 16 + 8 * yh] for c in range(2) for z in range(8)])
+    for offset in order:
+        dx, dy, dz = offset
+        if dx and not (dy and dz):
             side = 0 if dx > 0 else 1
             from_y, to_y, rows = tiles(dy)
             send(offset, PE.at[from_y, rows], RE.at[side, 1 - dz, to_y, rows], send_c, recv_c)
@@ -520,7 +520,7 @@
         coarse(zc, (4, 20), 1)
         return carry
 
-    lax.fori_loop(2, 10, own_planes, 0, unroll=4)
+    lax.fori_loop(2, 10, own_planes, 0, unroll=8)
     coarse(1, (8, 16), 1)
     coarse(10, (8, 16), 1)
 

time: 43.4 us -> 43.1 us (level)
  no operation moved by 1% of the time
where the time goes in v5:
time: 43.1 us; the launch traced here: 43 us
  Pallas kernels  42.3 us (98%)
  between operations  0.64 us (1%)
    pallas_call x1, Pallas kernels, shards(): pl.pallas_call(functools.partial(kernel, sizes), out_shape=(jax.ShapeDtyp...  41.6 us

profile of v5, /device:TPU:1, one launch (start us, length us, event | category | flops | bytes accessed | tf_op | source)
XLA Modules:
  0.0 43.0 jit_solution(5336488885429634777)
XLA Ops:
  0.6 41.6 %shard_map.85 = (f32[2,16,16,128]{3,2,1,0:T(8,128)S(1)}, f32[1,128]{1,0:T(1,128)S(1)}) custom-call(f32[2,16,16,128]{3,2,1,0:T(8,128)} %guess_hbm.1, f32[2,16,16,128]{3,2,1,0:T(8,128)} %source_hbm.1, f32[2,16,16,128]{3,2,1,0:T(8,128)} %forward_hbm.1, s32[16,16,128]{2,1,0:T(8,128)} %labels_hbm.1, f32[8]{0:T(128)} %pr_ref.1, f32[8]{0:T(128)} %pi_ref.1), custom_call_target="tpu_custom_call" | custom-call | tf_op jit(solution)/shard_map/pallas_call | solution.py:620
  42.2 0.7 %shard_map.86 = (f32[2,16,16,128]{3,2,1,0:T(8,128)}, f32[2,8]{1,0:T(2,128)}, f32[3]{0:T(128)}) custom-call(f32[2,16,16,128]{3,2,1,0:T(8,128)S(1)} %get-tuple-element.5.adjoint, f32[1,128]{1,0:T(1,128)S(1)} %get-tuple-element.6.row_ref), custom_call_target="tpu_custom_call" | custom-call | tf_op jit(solution)/shard_map/pallas_call | solution.py:667
